TPU v7x, 256 devices: a whole 4x4x8 slice. The times are simulated.
256 devices in a mesh: blk: 32 (over x, z_hi, y), head: 8 (over z_lo, core).
Axes of the slice: x: 4, y: 4, z: 8 (z_hi: 2, z_lo: 4; z = z_hi * 4 + z_lo), core: 2. Of those that a mesh axis runs over, the one named last changes fastest.
Arguments:
- queries: bfloat16 [2048, 64, 128], P(('blk', 'head')), may hold values from -12 to 12
- text_keyval: bfloat16 [32768, 8, 2, 128], P(('blk', 'head')), may hold values from -6 to 6
- visual_keyval: bfloat16 [12288, 8, 2, 128], P(('blk', 'head')), may hold values from -6 to 6
- visual_counts: int32 [256], replicated, may hold values from 1 to 95, as said below
Outputs:
- attended: bfloat16 [2048, 64, 128], P(('blk', 'head'))
Inputs may be any that keep to these rules, and one draw needn't show every extreme that they name: `visual_counts`: with d[o] = offsets[o + 1] - (o + 1) * 48: 0 <= d[o] < 48 for every device o, d of the next-to-last device is 47, d of the last device is 0, so the counts sum to 12288 and a device's visual rows lie in the visual blocks of itself and the next device.
All inputs are finite; a program needn't handle non-finite values.
Results may differ from a plain program's by a relative error of at most 0.018.
Values may be sent and summed in bfloat16 or wider, within the bound.
No kernel may reach another device: no remote copies, remote signals or barrier semaphores. Data moves between devices by JAX's collectives and lax.ppermute only.
A program may use at most 64 MiB of HBM per device.

v0:
```python
import math

import jax
import jax.numpy as jnp
from jax import lax
from jax.sharding import PartitionSpec as P


def from_behind(value, axis, steps):
    count = lax.axis_size(axis)
    first, last = (max(0, -steps), min(count, count - steps))
    return lax.ppermute(value, axis, [(source, source + steps) for source in range(first, last)])


def on_device(queries, text_keyval, visual_keyval, visual_counts):
    tok_rows = text_keyval.shape[0]
    vis_rows = visual_keyval.shape[0]
    query_rows = queries.shape[0]
    head_count = lax.axis_size("head")
    blk_count = lax.axis_size("blk")
    block_id = lax.axis_index("blk")
    owner_index = block_id * head_count + lax.axis_index("head")
    offsets = jnp.cumsum(visual_counts) - visual_counts
    visual_here = visual_counts[owner_index]
    window_start = offsets[owner_index] - owner_index * vis_rows
    following = from_behind(visual_keyval, ("blk", "head"), -1)
    padding = jnp.zeros((tok_rows,) + visual_keyval.shape[1:], jnp.bfloat16)
    stacked = jnp.concatenate([visual_keyval, following, padding], axis=0)
    window = lax.dynamic_slice_in_dim(stacked, window_start, tok_rows, 0)
    row_within = jnp.arange(tok_rows, dtype=jnp.int32)
    keyval = jnp.where((row_within < visual_here)[:, None, None, None], window, text_keyval)
    local_query, local_keyval = (
        lax.all_to_all(queries, "head", split_axis=1, concat_axis=0, tiled=True),
        lax.all_to_all(keyval, "head", split_axis=1, concat_axis=0, tiled=True),
    )
    query_count = local_query.shape[0]
    q_heads = local_query.shape[1]
    head_width = local_query.shape[2]
    kv_heads = local_keyval.shape[1]
    kv_rows = local_keyval.shape[0]
    group_size = q_heads // kv_heads
    grouped = local_query.reshape(query_count, kv_heads, group_size, head_width)
    score_scale = 1.0 / math.sqrt(head_width)
    query_order = jnp.arange(query_count, dtype=jnp.int32)
    query_place = (
        (block_id * head_count + query_order // query_rows) * tok_rows
        + tok_rows
        - query_rows
        + query_order % query_rows
    )

    def attend(status, block_kv, first_key):
        maxima, totals, weighted = status
        key_place = first_key + jnp.arange(block_kv.shape[0], dtype=jnp.int32)
        scores = (
            jnp.einsum(
                "rkgd,nkd->rkgn", grouped, block_kv[:, :, 0, :], preferred_element_type=jnp.float32
            )
            * score_scale
        )
        allowed = key_place[None, :] <= query_place[:, None]
        scores = jnp.where(allowed[:, None, None, :], scores, -1e30)
        new_maxima = jnp.maximum(maxima, jnp.max(scores, axis=3))
        rescale = jnp.exp(maxima - new_maxima)
        exponent = jnp.exp(scores - new_maxima[..., None])
        totals = totals * rescale + jnp.sum(exponent, axis=3)
        weights = exponent.astype(jnp.bfloat16)
        weighted = weighted * rescale[..., None] + jnp.einsum(
            "rkgn,nkd->rkgd", weights, block_kv[:, :, 1, :], preferred_element_type=jnp.float32
        )
        return (new_maxima, totals, weighted)

    def visit(status, block_kv, first_key):
        return attend(status, block_kv, first_key)

    status = (
        jnp.full((query_count, kv_heads, group_size), -1e30, jnp.float32),
        jnp.zeros((query_count, kv_heads, group_size), jnp.float32),
        jnp.zeros((query_count, kv_heads, group_size, head_width), jnp.float32),
    )
    status = visit(status, local_keyval, block_id * kv_rows)

    def cycle_step(turn_index, looped):
        inner, current = looped
        current = from_behind(current, "blk", 1)
        anchor = (block_id - turn_index) % blk_count
        inner = visit(inner, current, anchor * kv_rows)
        return (inner, current)

    status, _ = lax.fori_loop(1, blk_count, cycle_step, (status, local_keyval))
    maxima, totals, weighted = status
    attended = (weighted / totals[..., None]).astype(jnp.bfloat16)
    attended = attended.reshape(query_count, q_heads, head_width)
    return lax.all_to_all(attended, "head", split_axis=0, concat_axis=1, tiled=True)


def solution(mesh):
    in_specs = (
        P(("blk", "head"), None, None),
        P(("blk", "head"), None, None, None),
        P(("blk", "head"), None, None, None),
        P(),
    )
    out_specs = P(("blk", "head"), None, None)
    return jax.shard_map(
        on_device, mesh=mesh, in_specs=in_specs, out_specs=out_specs, check_vma=False
    )
```

profile of v0, /device:TPU:134, one launch (start us, length us, event | category | flops | bytes accessed | tf_op | source)
XLA Modules:
  0.0 1013.3 jit_solution(2603058741123155756)
XLA Ops:
  41.0 820.7 %while.22 = (s32[]{:T(128)}, f32[64,1,8]{0,2,1:T(8,128)S(1)}, f32[64,1,8]{0,2,1:T(8,128)S(1)}, f32[64,1,8,128]{3,0,2,1:T(8,128)S(1)}, bf16[1024,1,2,128]{3,0,2,1...) while((s32[]{:T(128)}, f32[64,1,8]{0,2,1:T(8,128)S(1)}, ...), condition=%wide.region_7.8_spmd.clone, body=%wide.region_4.7_spmd.clone.sunk | while | flops 272305664 | bytes 10793778 | solution.py:90
  43.9 18.6 %collective-permute-done = bf16[1024,1,2,128]{3,0,2,1:T(8,128)(2,1)S(1)} collective-permute-done((bf16[1024,1,2,128]{3,0,2,1:T(8,128)(2,1)S(1)}, bf16[1024,1,2,128]{3,0,2,1:T(8,128)(2,1)S(1)}, u32[]{:S(2)}, u32[]{:S(2)}) %collective-permute-start) | collective-permute-done | bytes 524320 | tf_op jit(solution)/shard_map/while/body/eval_jaxpr/ppermute | solution.py:12
  66.3 18.4 %collective-permute-done = bf16[1024,1,2,128]{3,0,2,1:T(8,128)(2,1)S(1)} collective-permute-done((bf16[1024,1,2,128]{3,0,2,1:T(8,128)(2,1)S(1)}, bf16[1024,1,2,128]{3,0,2,1:T(8,128)(2,1)S(1)}, u32[]{:S(2)}, u32[]{:S(2)}) %collective-permute-start) | collective-permute-done | bytes 524320 | tf_op jit(solution)/shard_map/while/body/eval_jaxpr/ppermute | solution.py:12
  88.5 17.4 %collective-permute-done = bf16[1024,1,2,128]{3,0,2,1:T(8,128)(2,1)S(1)} collective-permute-done((bf16[1024,1,2,128]{3,0,2,1:T(8,128)(2,1)S(1)}, bf16[1024,1,2,128]{3,0,2,1:T(8,128)(2,1)S(1)}, u32[]{:S(2)}, u32[]{:S(2)}) %collective-permute-start) | collective-permute-done | bytes 524320 | tf_op jit(solution)/shard_map/while/body/eval_jaxpr/ppermute | solution.py:12
  109.6 16.3 %collective-permute-done = bf16[1024,1,2,128]{3,0,2,1:T(8,128)(2,1)S(1)} collective-permute-done((bf16[1024,1,2,128]{3,0,2,1:T(8,128)(2,1)S(1)}, bf16[1024,1,2,128]{3,0,2,1:T(8,128)(2,1)S(1)}, u32[]{:S(2)}, u32[]{:S(2)}) %collective-permute-start) | collective-permute-done | bytes 524320 | tf_op jit(solution)/shard_map/while/body/eval_jaxpr/ppermute | solution.py:12
  129.8 15.3 %collective-permute-done = bf16[1024,1,2,128]{3,0,2,1:T(8,128)(2,1)S(1)} collective-permute-done((bf16[1024,1,2,128]{3,0,2,1:T(8,128)(2,1)S(1)}, bf16[1024,1,2,128]{3,0,2,1:T(8,128)(2,1)S(1)}, u32[]{:S(2)}, u32[]{:S(2)}) %collective-permute-start) | collective-permute-done | bytes 524320 | tf_op jit(solution)/shard_map/while/body/eval_jaxpr/ppermute | solution.py:12
  148.9 20.2 %collective-permute-done = bf16[1024,1,2,128]{3,0,2,1:T(8,128)(2,1)S(1)} collective-permute-done((bf16[1024,1,2,128]{3,0,2,1:T(8,128)(2,1)S(1)}, bf16[1024,1,2,128]{3,0,2,1:T(8,128)(2,1)S(1)}, u32[]{:S(2)}, u32[]{:S(2)}) %collective-permute-start) | collective-permute-done | bytes 524320 | tf_op jit(solution)/shard_map/while/body/eval_jaxpr/ppermute | solution.py:12
  172.9 23.4 %collective-permute-done = bf16[1024,1,2,128]{3,0,2,1:T(8,128)(2,1)S(1)} collective-permute-done((bf16[1024,1,2,128]{3,0,2,1:T(8,128)(2,1)S(1)}, bf16[1024,1,2,128]{3,0,2,1:T(8,128)(2,1)S(1)}, u32[]{:S(2)}, u32[]{:S(2)}) %collective-permute-start) | collective-permute-done | bytes 524320 | tf_op jit(solution)/shard_map/while/body/eval_jaxpr/ppermute | solution.py:12
  200.1 17.1 %collective-permute-done = bf16[1024,1,2,128]{3,0,2,1:T(8,128)(2,1)S(1)} collective-permute-done((bf16[1024,1,2,128]{3,0,2,1:T(8,128)(2,1)S(1)}, bf16[1024,1,2,128]{3,0,2,1:T(8,128)(2,1)S(1)}, u32[]{:S(2)}, u32[]{:S(2)}) %collective-permute-start) | collective-permute-done | bytes 524320 | tf_op jit(solution)/shard_map/while/body/eval_jaxpr/ppermute | solution.py:12
  221.0 21.3 %collective-permute-done = bf16[1024,1,2,128]{3,0,2,1:T(8,128)(2,1)S(1)} collective-permute-done((bf16[1024,1,2,128]{3,0,2,1:T(8,128)(2,1)S(1)}, bf16[1024,1,2,128]{3,0,2,1:T(8,128)(2,1)S(1)}, u32[]{:S(2)}, u32[]{:S(2)}) %collective-permute-start) | collective-permute-done | bytes 524320 | tf_op jit(solution)/shard_map/while/body/eval_jaxpr/ppermute | solution.py:12
  246.1 23.6 %collective-permute-done = bf16[1024,1,2,128]{3,0,2,1:T(8,128)(2,1)S(1)} collective-permute-done((bf16[1024,1,2,128]{3,0,2,1:T(8,128)(2,1)S(1)}, bf16[1024,1,2,128]{3,0,2,1:T(8,128)(2,1)S(1)}, u32[]{:S(2)}, u32[]{:S(2)}) %collective-permute-start) | collective-permute-done | bytes 524320 | tf_op jit(solution)/shard_map/while/body/eval_jaxpr/ppermute | solution.py:12
  273.5 18.6 %collective-permute-done = bf16[1024,1,2,128]{3,0,2,1:T(8,128)(2,1)S(1)} collective-permute-done((bf16[1024,1,2,128]{3,0,2,1:T(8,128)(2,1)S(1)}, bf16[1024,1,2,128]{3,0,2,1:T(8,128)(2,1)S(1)}, u32[]{:S(2)}, u32[]{:S(2)}) %collective-permute-start) | collective-permute-done | bytes 524320 | tf_op jit(solution)/shard_map/while/body/eval_jaxpr/ppermute | solution.py:12
  296.0 23.9 %collective-permute-done = bf16[1024,1,2,128]{3,0,2,1:T(8,128)(2,1)S(1)} collective-permute-done((bf16[1024,1,2,128]{3,0,2,1:T(8,128)(2,1)S(1)}, bf16[1024,1,2,128]{3,0,2,1:T(8,128)(2,1)S(1)}, u32[]{:S(2)}, u32[]{:S(2)}) %collective-permute-start) | collective-permute-done | bytes 524320 | tf_op jit(solution)/shard_map/while/body/eval_jaxpr/ppermute | solution.py:12
  323.7 18.4 %collective-permute-done = bf16[1024,1,2,128]{3,0,2,1:T(8,128)(2,1)S(1)} collective-permute-done((bf16[1024,1,2,128]{3,0,2,1:T(8,128)(2,1)S(1)}, bf16[1024,1,2,128]{3,0,2,1:T(8,128)(2,1)S(1)}, u32[]{:S(2)}, u32[]{:S(2)}) %collective-permute-start) | collective-permute-done | bytes 524320 | tf_op jit(solution)/shard_map/while/body/eval_jaxpr/ppermute | solution.py:12
  345.9 16.4 %collective-permute-done = bf16[1024,1,2,128]{3,0,2,1:T(8,128)(2,1)S(1)} collective-permute-done((bf16[1024,1,2,128]{3,0,2,1:T(8,128)(2,1)S(1)}, bf16[1024,1,2,128]{3,0,2,1:T(8,128)(2,1)S(1)}, u32[]{:S(2)}, u32[]{:S(2)}) %collective-permute-start) | collective-permute-done | bytes 524320 | tf_op jit(solution)/shard_map/while/body/eval_jaxpr/ppermute | solution.py:12
  366.1 28.8 %collective-permute-done = bf16[1024,1,2,128]{3,0,2,1:T(8,128)(2,1)S(1)} collective-permute-done((bf16[1024,1,2,128]{3,0,2,1:T(8,128)(2,1)S(1)}, bf16[1024,1,2,128]{3,0,2,1:T(8,128)(2,1)S(1)}, u32[]{:S(2)}, u32[]{:S(2)}) %collective-permute-start) | collective-permute-done | bytes 524320 | tf_op jit(solution)/shard_map/while/body/eval_jaxpr/ppermute | solution.py:12
  398.8 21.9 %collective-permute-done = bf16[1024,1,2,128]{3,0,2,1:T(8,128)(2,1)S(1)} collective-permute-done((bf16[1024,1,2,128]{3,0,2,1:T(8,128)(2,1)S(1)}, bf16[1024,1,2,128]{3,0,2,1:T(8,128)(2,1)S(1)}, u32[]{:S(2)}, u32[]{:S(2)}) %collective-permute-start) | collective-permute-done | bytes 524320 | tf_op jit(solution)/shard_map/while/body/eval_jaxpr/ppermute | solution.py:12
  424.5 23.5 %collective-permute-done = bf16[1024,1,2,128]{3,0,2,1:T(8,128)(2,1)S(1)} collective-permute-done((bf16[1024,1,2,128]{3,0,2,1:T(8,128)(2,1)S(1)}, bf16[1024,1,2,128]{3,0,2,1:T(8,128)(2,1)S(1)}, u32[]{:S(2)}, u32[]{:S(2)}) %collective-permute-start) | collective-permute-done | bytes 524320 | tf_op jit(solution)/shard_map/while/body/eval_jaxpr/ppermute | solution.py:12
  451.9 20.6 %collective-permute-done = bf16[1024,1,2,128]{3,0,2,1:T(8,128)(2,1)S(1)} collective-permute-done((bf16[1024,1,2,128]{3,0,2,1:T(8,128)(2,1)S(1)}, bf16[1024,1,2,128]{3,0,2,1:T(8,128)(2,1)S(1)}, u32[]{:S(2)}, u32[]{:S(2)}) %collective-permute-start) | collective-permute-done | bytes 524320 | tf_op jit(solution)/shard_map/while/body/eval_jaxpr/ppermute | solution.py:12
  476.4 22.7 %collective-permute-done = bf16[1024,1,2,128]{3,0,2,1:T(8,128)(2,1)S(1)} collective-permute-done((bf16[1024,1,2,128]{3,0,2,1:T(8,128)(2,1)S(1)}, bf16[1024,1,2,128]{3,0,2,1:T(8,128)(2,1)S(1)}, u32[]{:S(2)}, u32[]{:S(2)}) %collective-permute-start) | collective-permute-done | bytes 524320 | tf_op jit(solution)/shard_map/while/body/eval_jaxpr/ppermute | solution.py:12
  502.9 26.3 %collective-permute-done = bf16[1024,1,2,128]{3,0,2,1:T(8,128)(2,1)S(1)} collective-permute-done((bf16[1024,1,2,128]{3,0,2,1:T(8,128)(2,1)S(1)}, bf16[1024,1,2,128]{3,0,2,1:T(8,128)(2,1)S(1)}, u32[]{:S(2)}, u32[]{:S(2)}) %collective-permute-start) | collective-permute-done | bytes 524320 | tf_op jit(solution)/shard_map/while/body/eval_jaxpr/ppermute | solution.py:12
  533.0 22.5 %collective-permute-done = bf16[1024,1,2,128]{3,0,2,1:T(8,128)(2,1)S(1)} collective-permute-done((bf16[1024,1,2,128]{3,0,2,1:T(8,128)(2,1)S(1)}, bf16[1024,1,2,128]{3,0,2,1:T(8,128)(2,1)S(1)}, u32[]{:S(2)}, u32[]{:S(2)}) %collective-permute-start) | collective-permute-done | bytes 524320 | tf_op jit(solution)/shard_map/while/body/eval_jaxpr/ppermute | solution.py:12
  559.4 34.3 %collective-permute-done = bf16[1024,1,2,128]{3,0,2,1:T(8,128)(2,1)S(1)} collective-permute-done((bf16[1024,1,2,128]{3,0,2,1:T(8,128)(2,1)S(1)}, bf16[1024,1,2,128]{3,0,2,1:T(8,128)(2,1)S(1)}, u32[]{:S(2)}, u32[]{:S(2)}) %collective-permute-start) | collective-permute-done | bytes 524320 | tf_op jit(solution)/shard_map/while/body/eval_jaxpr/ppermute | solution.py:12
  597.5 26.2 %collective-permute-done = bf16[1024,1,2,128]{3,0,2,1:T(8,128)(2,1)S(1)} collective-permute-done((bf16[1024,1,2,128]{3,0,2,1:T(8,128)(2,1)S(1)}, bf16[1024,1,2,128]{3,0,2,1:T(8,128)(2,1)S(1)}, u32[]{:S(2)}, u32[]{:S(2)}) %collective-permute-start) | collective-permute-done | bytes 524320 | tf_op jit(solution)/shard_map/while/body/eval_jaxpr/ppermute | solution.py:12
  627.5 28.0 %collective-permute-done = bf16[1024,1,2,128]{3,0,2,1:T(8,128)(2,1)S(1)} collective-permute-done((bf16[1024,1,2,128]{3,0,2,1:T(8,128)(2,1)S(1)}, bf16[1024,1,2,128]{3,0,2,1:T(8,128)(2,1)S(1)}, u32[]{:S(2)}, u32[]{:S(2)}) %collective-permute-start) | collective-permute-done | bytes 524320 | tf_op jit(solution)/shard_map/while/body/eval_jaxpr/ppermute | solution.py:12
  659.4 24.4 %collective-permute-done = bf16[1024,1,2,128]{3,0,2,1:T(8,128)(2,1)S(1)} collective-permute-done((bf16[1024,1,2,128]{3,0,2,1:T(8,128)(2,1)S(1)}, bf16[1024,1,2,128]{3,0,2,1:T(8,128)(2,1)S(1)}, u32[]{:S(2)}, u32[]{:S(2)}) %collective-permute-start) | collective-permute-done | bytes 524320 | tf_op jit(solution)/shard_map/while/body/eval_jaxpr/ppermute | solution.py:12
  706.4 35.7 %collective-permute-done = bf16[1024,1,2,128]{3,0,2,1:T(8,128)(2,1)S(1)} collective-permute-done((bf16[1024,1,2,128]{3,0,2,1:T(8,128)(2,1)S(1)}, bf16[1024,1,2,128]{3,0,2,1:T(8,128)(2,1)S(1)}, u32[]{:S(2)}, u32[]{:S(2)}) %collective-permute-start) | collective-permute-done | bytes 524320 | tf_op jit(solution)/shard_map/while/body/eval_jaxpr/ppermute | solution.py:12
  746.0 27.8 %collective-permute-done = bf16[1024,1,2,128]{3,0,2,1:T(8,128)(2,1)S(1)} collective-permute-done((bf16[1024,1,2,128]{3,0,2,1:T(8,128)(2,1)S(1)}, bf16[1024,1,2,128]{3,0,2,1:T(8,128)(2,1)S(1)}, u32[]{:S(2)}, u32[]{:S(2)}) %collective-permute-start) | collective-permute-done | bytes 524320 | tf_op jit(solution)/shard_map/while/body/eval_jaxpr/ppermute | solution.py:12
  777.6 25.8 %collective-permute-done = bf16[1024,1,2,128]{3,0,2,1:T(8,128)(2,1)S(1)} collective-permute-done((bf16[1024,1,2,128]{3,0,2,1:T(8,128)(2,1)S(1)}, bf16[1024,1,2,128]{3,0,2,1:T(8,128)(2,1)S(1)}, u32[]{:S(2)}, u32[]{:S(2)}) %collective-permute-start) | collective-permute-done | bytes 524320 | tf_op jit(solution)/shard_map/while/body/eval_jaxpr/ppermute | solution.py:12
  807.2 26.4 %collective-permute-done = bf16[1024,1,2,128]{3,0,2,1:T(8,128)(2,1)S(1)} collective-permute-done((bf16[1024,1,2,128]{3,0,2,1:T(8,128)(2,1)S(1)}, bf16[1024,1,2,128]{3,0,2,1:T(8,128)(2,1)S(1)}, u32[]{:S(2)}, u32[]{:S(2)}) %collective-permute-start) | collective-permute-done | bytes 524320 | tf_op jit(solution)/shard_map/while/body/eval_jaxpr/ppermute | solution.py:12
  837.4 22.5 %collective-permute-done = bf16[1024,1,2,128]{3,0,2,1:T(8,128)(2,1)S(1)} collective-permute-done((bf16[1024,1,2,128]{3,0,2,1:T(8,128)(2,1)S(1)}, bf16[1024,1,2,128]{3,0,2,1:T(8,128)(2,1)S(1)}, u32[]{:S(2)}, u32[]{:S(2)}) %collective-permute-start) | collective-permute-done | bytes 524320 | tf_op jit(solution)/shard_map/while/body/eval_jaxpr/ppermute | solution.py:12
  861.9 150.7 %all_to_all.51 = bf16[64,8,128]{2,1,0:T(8,128)(2,1)S(1)} all-to-all(bf16[64,8,128]{2,1,0:T(8,128)(2,1)S(1)} %fusion.24), channel_id=1, replica_groups=mesh['blk'=32,'head'=8] {'head'}, dimensions={0} | all-to-all | bytes 262144 | tf_op jit(solution)/shard_map/all_to_all | solution.py:94
  (374 shorter events, 172.5 us)
Async XLA Ops:
  18.8 20.4 %all-to-all-start = ((bf16[128,8,2,128]{3,2,0,1:T(2,128)(2,1)}), bf16[128,8,2,128]{3,2,0,1:T(2,128)(2,1)S(1)}, u32[]{:S(2)}, u32[]{:S(2)}) async-start(bf16[128,8,2,128]{3,2,0,1:T(2,128)(2,1)} %broadcast_select_fusion), calls=%async_computation | async-start | bytes 1048576 | tf_op jit(solution)/shard_map/all_to_all | solution.py:34
  41.0 21.5 %collective-permute-start = (bf16[1024,1,2,128]{3,0,2,1:T(8,128)(2,1)S(1)}, bf16[1024,1,2,128]{3,0,2,1:T(8,128)(2,1)S(1)}, u32[]{:S(2)}, u32[]{:S(2)}) collective-permute-start(bf16[1024,1,2,128]{3,0,2,1:T(8,128)(2,1)S(1)} %get-tuple-element.341), channel_id=1, source_target_pairs={{0,8},{8,16},{16,24},{24,32},{32,40},{40,48},{48,56},{56,64},{64,7... | collective-permute-start | bytes 1572872 | tf_op jit(solution)/shard_map/while/body/eval_jaxpr/ppermute | solution.py:12
  64.2 20.5 %collective-permute-start = (bf16[1024,1,2,128]{3,0,2,1:T(8,128)(2,1)S(1)}, bf16[1024,1,2,128]{3,0,2,1:T(8,128)(2,1)S(1)}, u32[]{:S(2)}, u32[]{:S(2)}) collective-permute-start(bf16[1024,1,2,128]{3,0,2,1:T(8,128)(2,1)S(1)} %get-tuple-element.341), channel_id=1, source_target_pairs={{0,8},{8,16},{16,24},{24,32},{32,40},{40,48},{48,56},{56,64},{64,7... | collective-permute-start | bytes 1572872 | tf_op jit(solution)/shard_map/while/body/eval_jaxpr/ppermute | solution.py:12
  86.4 19.4 %collective-permute-start = (bf16[1024,1,2,128]{3,0,2,1:T(8,128)(2,1)S(1)}, bf16[1024,1,2,128]{3,0,2,1:T(8,128)(2,1)S(1)}, u32[]{:S(2)}, u32[]{:S(2)}) collective-permute-start(bf16[1024,1,2,128]{3,0,2,1:T(8,128)(2,1)S(1)} %get-tuple-element.341), channel_id=1, source_target_pairs={{0,8},{8,16},{16,24},{24,32},{32,40},{40,48},{48,56},{56,64},{64,7... | collective-permute-start | bytes 1572872 | tf_op jit(solution)/shard_map/while/body/eval_jaxpr/ppermute | solution.py:12
  107.6 18.4 %collective-permute-start = (bf16[1024,1,2,128]{3,0,2,1:T(8,128)(2,1)S(1)}, bf16[1024,1,2,128]{3,0,2,1:T(8,128)(2,1)S(1)}, u32[]{:S(2)}, u32[]{:S(2)}) collective-permute-start(bf16[1024,1,2,128]{3,0,2,1:T(8,128)(2,1)S(1)} %get-tuple-element.341), channel_id=1, source_target_pairs={{0,8},{8,16},{16,24},{24,32},{32,40},{40,48},{48,56},{56,64},{64,7... | collective-permute-start | bytes 1572872 | tf_op jit(solution)/shard_map/while/body/eval_jaxpr/ppermute | solution.py:12
  127.7 17.4 %collective-permute-start = (bf16[1024,1,2,128]{3,0,2,1:T(8,128)(2,1)S(1)}, bf16[1024,1,2,128]{3,0,2,1:T(8,128)(2,1)S(1)}, u32[]{:S(2)}, u32[]{:S(2)}) collective-permute-start(bf16[1024,1,2,128]{3,0,2,1:T(8,128)(2,1)S(1)} %get-tuple-element.341), channel_id=1, source_target_pairs={{0,8},{8,16},{16,24},{24,32},{32,40},{40,48},{48,56},{56,64},{64,7... | collective-permute-start | bytes 1572872 | tf_op jit(solution)/shard_map/while/body/eval_jaxpr/ppermute | solution.py:12
  146.8 22.3 %collective-permute-start = (bf16[1024,1,2,128]{3,0,2,1:T(8,128)(2,1)S(1)}, bf16[1024,1,2,128]{3,0,2,1:T(8,128)(2,1)S(1)}, u32[]{:S(2)}, u32[]{:S(2)}) collective-permute-start(bf16[1024,1,2,128]{3,0,2,1:T(8,128)(2,1)S(1)} %get-tuple-element.341), channel_id=1, source_target_pairs={{0,8},{8,16},{16,24},{24,32},{32,40},{40,48},{48,56},{56,64},{64,7... | collective-permute-start | bytes 1572872 | tf_op jit(solution)/shard_map/while/body/eval_jaxpr/ppermute | solution.py:12
  170.8 25.5 %collective-permute-start = (bf16[1024,1,2,128]{3,0,2,1:T(8,128)(2,1)S(1)}, bf16[1024,1,2,128]{3,0,2,1:T(8,128)(2,1)S(1)}, u32[]{:S(2)}, u32[]{:S(2)}) collective-permute-start(bf16[1024,1,2,128]{3,0,2,1:T(8,128)(2,1)S(1)} %get-tuple-element.341), channel_id=1, source_target_pairs={{0,8},{8,16},{16,24},{24,32},{32,40},{40,48},{48,56},{56,64},{64,7... | collective-permute-start | bytes 1572872 | tf_op jit(solution)/shard_map/while/body/eval_jaxpr/ppermute | solution.py:12
  198.0 19.2 %collective-permute-start = (bf16[1024,1,2,128]{3,0,2,1:T(8,128)(2,1)S(1)}, bf16[1024,1,2,128]{3,0,2,1:T(8,128)(2,1)S(1)}, u32[]{:S(2)}, u32[]{:S(2)}) collective-permute-start(bf16[1024,1,2,128]{3,0,2,1:T(8,128)(2,1)S(1)} %get-tuple-element.341), channel_id=1, source_target_pairs={{0,8},{8,16},{16,24},{24,32},{32,40},{40,48},{48,56},{56,64},{64,7... | collective-permute-start | bytes 1572872 | tf_op jit(solution)/shard_map/while/body/eval_jaxpr/ppermute | solution.py:12
  218.9 23.3 %collective-permute-start = (bf16[1024,1,2,128]{3,0,2,1:T(8,128)(2,1)S(1)}, bf16[1024,1,2,128]{3,0,2,1:T(8,128)(2,1)S(1)}, u32[]{:S(2)}, u32[]{:S(2)}) collective-permute-start(bf16[1024,1,2,128]{3,0,2,1:T(8,128)(2,1)S(1)} %get-tuple-element.341), channel_id=1, source_target_pairs={{0,8},{8,16},{16,24},{24,32},{32,40},{40,48},{48,56},{56,64},{64,7... | collective-permute-start | bytes 1572872 | tf_op jit(solution)/shard_map/while/body/eval_jaxpr/ppermute | solution.py:12
  244.0 25.7 %collective-permute-start = (bf16[1024,1,2,128]{3,0,2,1:T(8,128)(2,1)S(1)}, bf16[1024,1,2,128]{3,0,2,1:T(8,128)(2,1)S(1)}, u32[]{:S(2)}, u32[]{:S(2)}) collective-permute-start(bf16[1024,1,2,128]{3,0,2,1:T(8,128)(2,1)S(1)} %get-tuple-element.341), channel_id=1, source_target_pairs={{0,8},{8,16},{16,24},{24,32},{32,40},{40,48},{48,56},{56,64},{64,7... | collective-permute-start | bytes 1572872 | tf_op jit(solution)/shard_map/while/body/eval_jaxpr/ppermute | solution.py:12
  271.5 20.7 %collective-permute-start = (bf16[1024,1,2,128]{3,0,2,1:T(8,128)(2,1)S(1)}, bf16[1024,1,2,128]{3,0,2,1:T(8,128)(2,1)S(1)}, u32[]{:S(2)}, u32[]{:S(2)}) collective-permute-start(bf16[1024,1,2,128]{3,0,2,1:T(8,128)(2,1)S(1)} %get-tuple-element.341), channel_id=1, source_target_pairs={{0,8},{8,16},{16,24},{24,32},{32,40},{40,48},{48,56},{56,64},{64,7... | collective-permute-start | bytes 1572872 | tf_op jit(solution)/shard_map/while/body/eval_jaxpr/ppermute | solution.py:12
  293.9 26.0 %collective-permute-start = (bf16[1024,1,2,128]{3,0,2,1:T(8,128)(2,1)S(1)}, bf16[1024,1,2,128]{3,0,2,1:T(8,128)(2,1)S(1)}, u32[]{:S(2)}, u32[]{:S(2)}) collective-permute-start(bf16[1024,1,2,128]{3,0,2,1:T(8,128)(2,1)S(1)} %get-tuple-element.341), channel_id=1, source_target_pairs={{0,8},{8,16},{16,24},{24,32},{32,40},{40,48},{48,56},{56,64},{64,7... | collective-permute-start | bytes 1572872 | tf_op jit(solution)/shard_map/while/body/eval_jaxpr/ppermute | solution.py:12
  321.6 20.5 %collective-permute-start = (bf16[1024,1,2,128]{3,0,2,1:T(8,128)(2,1)S(1)}, bf16[1024,1,2,128]{3,0,2,1:T(8,128)(2,1)S(1)}, u32[]{:S(2)}, u32[]{:S(2)}) collective-permute-start(bf16[1024,1,2,128]{3,0,2,1:T(8,128)(2,1)S(1)} %get-tuple-element.341), channel_id=1, source_target_pairs={{0,8},{8,16},{16,24},{24,32},{32,40},{40,48},{48,56},{56,64},{64,7... | collective-permute-start | bytes 1572872 | tf_op jit(solution)/shard_map/while/body/eval_jaxpr/ppermute | solution.py:12
  343.8 18.5 %collective-permute-start = (bf16[1024,1,2,128]{3,0,2,1:T(8,128)(2,1)S(1)}, bf16[1024,1,2,128]{3,0,2,1:T(8,128)(2,1)S(1)}, u32[]{:S(2)}, u32[]{:S(2)}) collective-permute-start(bf16[1024,1,2,128]{3,0,2,1:T(8,128)(2,1)S(1)} %get-tuple-element.341), channel_id=1, source_target_pairs={{0,8},{8,16},{16,24},{24,32},{32,40},{40,48},{48,56},{56,64},{64,7... | collective-permute-start | bytes 1572872 | tf_op jit(solution)/shard_map/while/body/eval_jaxpr/ppermute | solution.py:12
  364.0 30.9 %collective-permute-start = (bf16[1024,1,2,128]{3,0,2,1:T(8,128)(2,1)S(1)}, bf16[1024,1,2,128]{3,0,2,1:T(8,128)(2,1)S(1)}, u32[]{:S(2)}, u32[]{:S(2)}) collective-permute-start(bf16[1024,1,2,128]{3,0,2,1:T(8,128)(2,1)S(1)} %get-tuple-element.341), channel_id=1, source_target_pairs={{0,8},{8,16},{16,24},{24,32},{32,40},{40,48},{48,56},{56,64},{64,7... | collective-permute-start | bytes 1572872 | tf_op jit(solution)/shard_map/while/body/eval_jaxpr/ppermute | solution.py:12
  396.7 24.0 %collective-permute-start = (bf16[1024,1,2,128]{3,0,2,1:T(8,128)(2,1)S(1)}, bf16[1024,1,2,128]{3,0,2,1:T(8,128)(2,1)S(1)}, u32[]{:S(2)}, u32[]{:S(2)}) collective-permute-start(bf16[1024,1,2,128]{3,0,2,1:T(8,128)(2,1)S(1)} %get-tuple-element.341), channel_id=1, source_target_pairs={{0,8},{8,16},{16,24},{24,32},{32,40},{40,48},{48,56},{56,64},{64,7... | collective-permute-start | bytes 1572872 | tf_op jit(solution)/shard_map/while/body/eval_jaxpr/ppermute | solution.py:12
  422.5 25.6 %collective-permute-start = (bf16[1024,1,2,128]{3,0,2,1:T(8,128)(2,1)S(1)}, bf16[1024,1,2,128]{3,0,2,1:T(8,128)(2,1)S(1)}, u32[]{:S(2)}, u32[]{:S(2)}) collective-permute-start(bf16[1024,1,2,128]{3,0,2,1:T(8,128)(2,1)S(1)} %get-tuple-element.341), channel_id=1, source_target_pairs={{0,8},{8,16},{16,24},{24,32},{32,40},{40,48},{48,56},{56,64},{64,7... | collective-permute-start | bytes 1572872 | tf_op jit(solution)/shard_map/while/body/eval_jaxpr/ppermute | solution.py:12
  449.8 22.7 %collective-permute-start = (bf16[1024,1,2,128]{3,0,2,1:T(8,128)(2,1)S(1)}, bf16[1024,1,2,128]{3,0,2,1:T(8,128)(2,1)S(1)}, u32[]{:S(2)}, u32[]{:S(2)}) collective-permute-start(bf16[1024,1,2,128]{3,0,2,1:T(8,128)(2,1)S(1)} %get-tuple-element.341), channel_id=1, source_target_pairs={{0,8},{8,16},{16,24},{24,32},{32,40},{40,48},{48,56},{56,64},{64,7... | collective-permute-start | bytes 1572872 | tf_op jit(solution)/shard_map/while/body/eval_jaxpr/ppermute | solution.py:12
  474.3 24.8 %collective-permute-start = (bf16[1024,1,2,128]{3,0,2,1:T(8,128)(2,1)S(1)}, bf16[1024,1,2,128]{3,0,2,1:T(8,128)(2,1)S(1)}, u32[]{:S(2)}, u32[]{:S(2)}) collective-permute-start(bf16[1024,1,2,128]{3,0,2,1:T(8,128)(2,1)S(1)} %get-tuple-element.341), channel_id=1, source_target_pairs={{0,8},{8,16},{16,24},{24,32},{32,40},{40,48},{48,56},{56,64},{64,7... | collective-permute-start | bytes 1572872 | tf_op jit(solution)/shard_map/while/body/eval_jaxpr/ppermute | solution.py:12
  500.8 28.4 %collective-permute-start = (bf16[1024,1,2,128]{3,0,2,1:T(8,128)(2,1)S(1)}, bf16[1024,1,2,128]{3,0,2,1:T(8,128)(2,1)S(1)}, u32[]{:S(2)}, u32[]{:S(2)}) collective-permute-start(bf16[1024,1,2,128]{3,0,2,1:T(8,128)(2,1)S(1)} %get-tuple-element.341), channel_id=1, source_target_pairs={{0,8},{8,16},{16,24},{24,32},{32,40},{40,48},{48,56},{56,64},{64,7... | collective-permute-start | bytes 1572872 | tf_op jit(solution)/shard_map/while/body/eval_jaxpr/ppermute | solution.py:12
  530.9 24.6 %collective-permute-start = (bf16[1024,1,2,128]{3,0,2,1:T(8,128)(2,1)S(1)}, bf16[1024,1,2,128]{3,0,2,1:T(8,128)(2,1)S(1)}, u32[]{:S(2)}, u32[]{:S(2)}) collective-permute-start(bf16[1024,1,2,128]{3,0,2,1:T(8,128)(2,1)S(1)} %get-tuple-element.341), channel_id=1, source_target_pairs={{0,8},{8,16},{16,24},{24,32},{32,40},{40,48},{48,56},{56,64},{64,7... | collective-permute-start | bytes 1572872 | tf_op jit(solution)/shard_map/while/body/eval_jaxpr/ppermute | solution.py:12
  557.3 36.4 %collective-permute-start = (bf16[1024,1,2,128]{3,0,2,1:T(8,128)(2,1)S(1)}, bf16[1024,1,2,128]{3,0,2,1:T(8,128)(2,1)S(1)}, u32[]{:S(2)}, u32[]{:S(2)}) collective-permute-start(bf16[1024,1,2,128]{3,0,2,1:T(8,128)(2,1)S(1)} %get-tuple-element.341), channel_id=1, source_target_pairs={{0,8},{8,16},{16,24},{24,32},{32,40},{40,48},{48,56},{56,64},{64,7... | collective-permute-start | bytes 1572872 | tf_op jit(solution)/shard_map/while/body/eval_jaxpr/ppermute | solution.py:12
  595.4 28.3 %collective-permute-start = (bf16[1024,1,2,128]{3,0,2,1:T(8,128)(2,1)S(1)}, bf16[1024,1,2,128]{3,0,2,1:T(8,128)(2,1)S(1)}, u32[]{:S(2)}, u32[]{:S(2)}) collective-permute-start(bf16[1024,1,2,128]{3,0,2,1:T(8,128)(2,1)S(1)} %get-tuple-element.341), channel_id=1, source_target_pairs={{0,8},{8,16},{16,24},{24,32},{32,40},{40,48},{48,56},{56,64},{64,7... | collective-permute-start | bytes 1572872 | tf_op jit(solution)/shard_map/while/body/eval_jaxpr/ppermute | solution.py:12
  625.4 30.1 %collective-permute-start = (bf16[1024,1,2,128]{3,0,2,1:T(8,128)(2,1)S(1)}, bf16[1024,1,2,128]{3,0,2,1:T(8,128)(2,1)S(1)}, u32[]{:S(2)}, u32[]{:S(2)}) collective-permute-start(bf16[1024,1,2,128]{3,0,2,1:T(8,128)(2,1)S(1)} %get-tuple-element.341), channel_id=1, source_target_pairs={{0,8},{8,16},{16,24},{24,32},{32,40},{40,48},{48,56},{56,64},{64,7... | collective-permute-start | bytes 1572872 | tf_op jit(solution)/shard_map/while/body/eval_jaxpr/ppermute | solution.py:12
  657.3 26.5 %collective-permute-start = (bf16[1024,1,2,128]{3,0,2,1:T(8,128)(2,1)S(1)}, bf16[1024,1,2,128]{3,0,2,1:T(8,128)(2,1)S(1)}, u32[]{:S(2)}, u32[]{:S(2)}) collective-permute-start(bf16[1024,1,2,128]{3,0,2,1:T(8,128)(2,1)S(1)} %get-tuple-element.341), channel_id=1, source_target_pairs={{0,8},{8,16},{16,24},{24,32},{32,40},{40,48},{48,56},{56,64},{64,7... | collective-permute-start | bytes 1572872 | tf_op jit(solution)/shard_map/while/body/eval_jaxpr/ppermute | solution.py:12
  685.5 17.1 %collective-permute-start = (bf16[1024,1,2,128]{3,0,2,1:T(8,128)(2,1)S(1)}, bf16[1024,1,2,128]{3,0,2,1:T(8,128)(2,1)S(1)}, u32[]{:S(2)}, u32[]{:S(2)}) collective-permute-start(bf16[1024,1,2,128]{3,0,2,1:T(8,128)(2,1)S(1)} %get-tuple-element.341), channel_id=1, source_target_pairs={{0,8},{8,16},{16,24},{24,32},{32,40},{40,48},{48,56},{56,64},{64,7... | collective-permute-start | bytes 1572872 | tf_op jit(solution)/shard_map/while/body/eval_jaxpr/ppermute | solution.py:12
  704.4 37.8 %collective-permute-start = (bf16[1024,1,2,128]{3,0,2,1:T(8,128)(2,1)S(1)}, bf16[1024,1,2,128]{3,0,2,1:T(8,128)(2,1)S(1)}, u32[]{:S(2)}, u32[]{:S(2)}) collective-permute-start(bf16[1024,1,2,128]{3,0,2,1:T(8,128)(2,1)S(1)} %get-tuple-element.341), channel_id=1, source_target_pairs={{0,8},{8,16},{16,24},{24,32},{32,40},{40,48},{48,56},{56,64},{64,7... | collective-permute-start | bytes 1572872 | tf_op jit(solution)/shard_map/while/body/eval_jaxpr/ppermute | solution.py:12
  743.9 29.9 %collective-permute-start = (bf16[1024,1,2,128]{3,0,2,1:T(8,128)(2,1)S(1)}, bf16[1024,1,2,128]{3,0,2,1:T(8,128)(2,1)S(1)}, u32[]{:S(2)}, u32[]{:S(2)}) collective-permute-start(bf16[1024,1,2,128]{3,0,2,1:T(8,128)(2,1)S(1)} %get-tuple-element.341), channel_id=1, source_target_pairs={{0,8},{8,16},{16,24},{24,32},{32,40},{40,48},{48,56},{56,64},{64,7... | collective-permute-start | bytes 1572872 | tf_op jit(solution)/shard_map/while/body/eval_jaxpr/ppermute | solution.py:12
  775.5 27.9 %collective-permute-start = (bf16[1024,1,2,128]{3,0,2,1:T(8,128)(2,1)S(1)}, bf16[1024,1,2,128]{3,0,2,1:T(8,128)(2,1)S(1)}, u32[]{:S(2)}, u32[]{:S(2)}) collective-permute-start(bf16[1024,1,2,128]{3,0,2,1:T(8,128)(2,1)S(1)} %get-tuple-element.341), channel_id=1, source_target_pairs={{0,8},{8,16},{16,24},{24,32},{32,40},{40,48},{48,56},{56,64},{64,7... | collective-permute-start | bytes 1572872 | tf_op jit(solution)/shard_map/while/body/eval_jaxpr/ppermute | solution.py:12
  805.1 28.5 %collective-permute-start = (bf16[1024,1,2,128]{3,0,2,1:T(8,128)(2,1)S(1)}, bf16[1024,1,2,128]{3,0,2,1:T(8,128)(2,1)S(1)}, u32[]{:S(2)}, u32[]{:S(2)}) collective-permute-start(bf16[1024,1,2,128]{3,0,2,1:T(8,128)(2,1)S(1)} %get-tuple-element.341), channel_id=1, source_target_pairs={{0,8},{8,16},{16,24},{24,32},{32,40},{40,48},{48,56},{56,64},{64,7... | collective-permute-start | bytes 1572872 | tf_op jit(solution)/shard_map/while/body/eval_jaxpr/ppermute | solution.py:12
  835.4 24.6 %collective-permute-start = (bf16[1024,1,2,128]{3,0,2,1:T(8,128)(2,1)S(1)}, bf16[1024,1,2,128]{3,0,2,1:T(8,128)(2,1)S(1)}, u32[]{:S(2)}, u32[]{:S(2)}) collective-permute-start(bf16[1024,1,2,128]{3,0,2,1:T(8,128)(2,1)S(1)} %get-tuple-element.341), channel_id=1, source_target_pairs={{0,8},{8,16},{16,24},{24,32},{32,40},{40,48},{48,56},{56,64},{64,7... | collective-permute-start | bytes 1572872 | tf_op jit(solution)/shard_map/while/body/eval_jaxpr/ppermute | solution.py:12
  (2 other events, 26.4 us)
where the time goes:
time: 1010 us
  waiting for transfers between devices  717 us (71%)
  blocking collectives  151 us (15%)
  starting transfers between devices  72.6 us (7%)
  matrix products  35.4 us (4%)
  other arithmetic  27.2 us (3%)
    ppermute x32, waiting for transfers between devices, from_behind(): lax.ppermute(value, axis, [(source, source + steps) for source in range(f...  701 us
    all_to_all x1, blocking collectives, on_device(): lax.all_to_all(attended, 'head', split_axis=0, concat_axis=1, tiled=True)  151 us
    ppermute x32, starting transfers between devices, from_behind(): lax.ppermute(value, axis, [(source, source + steps) for source in range(f...  64.3 us
  transfers between devices with their start and end apart: 34, of which 32 were waited for; matrix products, arithmetic and copies ran while one was open for 1% of the time, Pallas kernels for 0%

commit v1 on v0

v1 whole, which is shorter than its diff:
```python
import functools
import math

import jax
import jax.numpy as jnp
from jax import lax
from jax.experimental import pallas as pl
from jax.experimental.pallas import tpu as pltpu
from jax.sharding import Mesh, PartitionSpec as P

AXES = ("x", "zh", "y", "k", "zp", "c")
SIZES = (4, 2, 4, 2, 2, 2)
KEY_GROUP = ("x", "y", "zp")
QUERY_GROUP = ("x", "zh", "k", "zp")
NEVER = -1e30
VMEM = pl.BlockSpec(memory_space=pltpu.VMEM)


def place_kernel(counts_ref, text_ref, vis_ref, next_ref, send_ref, stacked):
    tok_rows = text_ref.shape[0] // 16
    vis_rows = vis_ref.shape[0] // 16
    owner = 0
    for axis, size in zip(AXES, SIZES):
        owner = owner * size + lax.axis_index(axis)
    counts = counts_ref[...].astype(jnp.float32)
    order = lax.broadcasted_iota(jnp.int32, counts.shape, 0) * 128 + lax.broadcasted_iota(
        jnp.int32, counts.shape, 1
    )
    before = jnp.sum(jnp.where(order < owner, counts, 0.0)).astype(jnp.int32)
    here = jnp.sum(jnp.where(order == owner, counts, 0.0)).astype(jnp.int32)
    start = jnp.clip(before - owner * vis_rows, 0, vis_rows - 1)
    stacked[0 : vis_rows * 16] = vis_ref[...]
    stacked[vis_rows * 16 : vis_rows * 32] = next_ref[...]
    out_row = lax.broadcasted_iota(jnp.int32, (256, 256), 0)
    in_row = lax.broadcasted_iota(jnp.int32, (256, 256), 1)
    to_heads = jnp.where(in_row == (out_row % 16) * 16 + out_row // 16, 1.0, 0.0)
    to_heads = to_heads.astype(jnp.bfloat16)
    row_within = lax.broadcasted_iota(jnp.int32, (256, 128), 0) // 16
    for part in range(tok_rows // 16):
        data = text_ref[part * 256 : (part + 1) * 256]
        if part * 16 < vis_rows * 2:
            window = stacked[pl.ds(pl.multiple_of(start * 16 + part * 256, 16), 256)]
            data = jnp.where(
                row_within + part * 16 < here, window.astype(jnp.float32), data.astype(jnp.float32)
            ).astype(jnp.bfloat16)
        moved = jnp.dot(to_heads, data, preferred_element_type=jnp.float32).astype(jnp.bfloat16)
        for head in range(8):
            for kind in range(2):
                slab = moved[(head * 2 + kind) * 16 : (head * 2 + kind + 1) * 16]
                for y in range(4):
                    send_ref[head // 2, y, head % 2, kind, part * 16 : (part + 1) * 16] = slab


def query_kernel(q_ref, send_ref):
    for pair in range(4):
        both = q_ref[:, pair * 16 : (pair + 1) * 16, :].astype(jnp.float32)
        for zp in range(2):
            chunk = both[:, zp * 8 : (zp + 1) * 8, :].reshape(64, 128).astype(jnp.bfloat16)
            for zh in range(2):
                for k in range(2):
                    send_ref[pair, zh, k, zp] = chunk


ROWS = 256


def attend_kernel(last, *refs):
    if last:
        q_ref, kv_ref, acc_in, m_in, send_ref = refs
    else:
        q_ref, kv_ref, acc_ref, m_ref = refs
    me = {axis: lax.axis_index(axis) for axis in ("zh", "y", "k", "c")}
    other = 1 - me["c"] if last else me["c"]
    scale = math.log2(math.e) / math.sqrt(128)
    ones = jnp.ones((1024, 128), jnp.bfloat16)

    def tile(xq, step):
        first = step * ROWS
        rows = pl.ds(pl.multiple_of(xq * 512 + first, ROWS), ROWS)
        scaled = q_ref[rows].astype(jnp.float32) * scale
        high = scaled.astype(jnp.bfloat16)
        low = (scaled - high.astype(jnp.float32)).astype(jnp.bfloat16)
        query = jnp.concatenate([high, low], axis=1)
        row = lax.broadcasted_iota(jnp.int32, (ROWS, 128), 0) + first
        lane = lax.broadcasted_iota(jnp.int32, (ROWS, 128), 1)
        z = row // 64
        q_dev = (z // 4) * 32 + me["y"] * 8 + ((z // 2) % 2) * 4 + (z % 2) * 2 + me["c"]
        reach = q_dev * 128 + 120 + (row % 64) // 8 - lane
        if last:
            maxima, acc = m_in[rows], acc_in[rows]
        for xk in range(xq + 1):
            keys = kv_ref[xk * 8 : (xk + 1) * 8, 0].reshape(1024, 128)
            values = kv_ref[xk * 8 : (xk + 1) * 8, 1].reshape(1024, 128)
            scores = lax.dot_general(
                query,
                jnp.concatenate([keys, keys], axis=1),
                (((1,), (1,)), ((), ())),
                preferred_element_type=jnp.float32,
            )
            parts = [scores[:, j * 128 : (j + 1) * 128] for j in range(8)]
            if xk == xq:
                for j in range(8):
                    k_dev = me["zh"] * 32 + (j // 2) * 8 + me["k"] * 4 + (j % 2) * 2 + other
                    parts[j] = jnp.where(reach >= k_dev * 128, parts[j], NEVER)
            top = functools.reduce(jnp.maximum, parts)
            top = jnp.max(top, axis=1, keepdims=True)
            if xk == 0 and not last:
                new = jnp.broadcast_to(top, (ROWS, 128))
            else:
                new = jnp.maximum(maxima, top)
            weights = jnp.concatenate(
                [jnp.exp2(part - new).astype(jnp.bfloat16) for part in parts], axis=1
            )
            added = jnp.dot(
                weights,
                jnp.concatenate([values, ones], axis=1),
                preferred_element_type=jnp.float32,
            )
            if xk == 0 and not last:
                acc = added
            else:
                shrink = jnp.exp2(maxima - new)
                acc = acc * jnp.concatenate([shrink, shrink], axis=1) + added
            maxima = new
        if not last:
            m_ref[rows] = maxima
            acc_ref[rows] = acc
            return
        totals = acc[:, 128:]
        result = (acc[:, :128] / totals).astype(jnp.bfloat16)
        level = maxima + jnp.log2(totals)
        eye = lax.broadcasted_iota(jnp.int32, (64, 128), 0) == lax.broadcasted_iota(
            jnp.int32, (64, 128), 1
        )
        stat_row = lax.broadcasted_iota(jnp.int32, (16, 128), 0)
        for j in range(ROWS // 64):
            chunk = xq * 8 + step * (ROWS // 64) + j
            send_ref[chunk, :64] = result[j * 64 : (j + 1) * 64]
            line = jnp.sum(
                jnp.where(eye, level[j * 64 : (j + 1) * 64], 0.0), axis=0, keepdims=True
            )
            one = line.astype(jnp.bfloat16).astype(jnp.float32)
            two = (line - one).astype(jnp.bfloat16).astype(jnp.float32)
            three = line - one - two
            stats = jnp.where(
                stat_row == 0, one, jnp.where(stat_row == 1, two, jnp.where(stat_row == 2, three, 0.0))
            )
            send_ref[chunk, 64:80] = stats.astype(jnp.bfloat16)

    for xq in range(4):
        @pl.loop(0, 512 // ROWS)
        def _(step):
            tile(xq, step)


def combine_kernel(recv_ref, out_ref):
    eye = lax.broadcasted_iota(jnp.int32, (64, 128), 0) == lax.broadcasted_iota(
        jnp.int32, (64, 128), 1
    )
    for x in range(4):
        heads = []
        for zp in range(2):
            chunks = [x * 8 + part * 2 + zp for part in range(4)]
            levels = []
            for chunk in chunks:
                stats = recv_ref[chunk, 64:80].astype(jnp.float32)
                levels.append(stats[0:1] + stats[1:2] + stats[2:3])
            top = functools.reduce(jnp.maximum, levels)
            shares = [jnp.exp2(level - top) for level in levels]
            whole = functools.reduce(jnp.add, shares)
            total = None
            for chunk, share in zip(chunks, shares):
                column = jnp.sum(jnp.where(eye, share / whole, 0.0), axis=1, keepdims=True)
                term = recv_ref[chunk, :64].astype(jnp.float32) * column
                total = term if total is None else total + term
            heads.append(total.reshape(8, 8, 128))
        out_ref[:, x * 16 : (x + 1) * 16, :] = jnp.concatenate(heads, axis=1).astype(jnp.bfloat16)


def params():
    return pltpu.CompilerParams(vmem_limit_bytes=32 * 1024 * 1024)


def on_device(queries, text_keyval, visual_keyval, visual_counts):
    owners = math.prod(SIZES)
    following = lax.ppermute(visual_keyval, AXES, [(i, i - 1) for i in range(1, owners)])
    q_send = pl.pallas_call(
        query_kernel,
        out_shape=jax.ShapeDtypeStruct((4, 2, 2, 2, 64, 128), jnp.bfloat16),
        in_specs=[VMEM],
        out_specs=VMEM,
        compiler_params=params(),
        name="query_chunks",
    )(queries)
    q_all = lax.all_to_all(q_send.reshape(32, 64, 128), QUERY_GROUP, 0, 0, tiled=True)
    q_all = q_all.reshape(2048, 128)
    kv_send = pl.pallas_call(
        place_kernel,
        out_shape=jax.ShapeDtypeStruct((4, 4, 2, 2, 128, 128), jnp.bfloat16),
        in_specs=[VMEM] * 4,
        out_specs=VMEM,
        scratch_shapes=[pltpu.VMEM((48 * 3 * 16, 128), jnp.bfloat16)],
        compiler_params=params(),
        name="place_rows",
    )(
        visual_counts.reshape(2, 128),
        text_keyval.reshape(2048, 128),
        visual_keyval.reshape(768, 128),
        following.reshape(768, 128),
    )
    kv_own = lax.all_to_all(kv_send.reshape(32, 2, 128, 128), KEY_GROUP, 0, 0, tiled=True)
    kv_other = lax.ppermute(kv_own, "c", [(0, 1), (1, 0)])
    acc, maxima = pl.pallas_call(
        functools.partial(attend_kernel, False),
        out_shape=(
            jax.ShapeDtypeStruct((2048, 256), jnp.float32),
            jax.ShapeDtypeStruct((2048, 128), jnp.float32),
        ),
        in_specs=[VMEM] * 2,
        out_specs=(VMEM, VMEM),
        compiler_params=params(),
        cost_estimate=pl.CostEstimate(
            flops=4 * 5242880 * 256, bytes_accessed=6 * 2**20, transcendentals=5242880
        ),
        name="attend_first",
    )(q_all, kv_own)
    o_send = pl.pallas_call(
        functools.partial(attend_kernel, True),
        out_shape=jax.ShapeDtypeStruct((32, 80, 128), jnp.bfloat16),
        in_specs=[VMEM] * 4,
        out_specs=VMEM,
        compiler_params=params(),
        name="attend_last",
    )(q_all, kv_other, acc, maxima)
    o_recv = lax.all_to_all(o_send, QUERY_GROUP, 0, 0, tiled=True)
    return pl.pallas_call(
        combine_kernel,
        out_shape=jax.ShapeDtypeStruct((8, 64, 128), jnp.bfloat16),
        in_specs=[VMEM],
        out_specs=VMEM,
        compiler_params=params(),
        name="combine_parts",
    )(o_recv)


def solution(mesh):
    fine = Mesh(mesh.devices.reshape(SIZES), AXES)
    in_specs = (
        P(AXES, None, None),
        P(AXES, None, None, None),
        P(AXES, None, None, None),
        P(),
    )
    out_specs = P(AXES, None, None)
    return jax.shard_map(
        on_device, mesh=fine, in_specs=in_specs, out_specs=out_specs, check_vma=False
    )
```

time: 1010 us -> 130 us (0.13)
  the two profiles are of different devices: /device:TPU:134 before, /device:TPU:32 now
where the time goes in v1:
time: 130 us; the launch traced here: 129 us
  blocking collectives  93.2 us (72%)
  Pallas kernels  28 us (22%)
  waiting for transfers between devices  3.48 us (3%)
  local copies, waits for them, and re-layouts  2.65 us (2%)
  starting transfers between devices  1.91 us (1%)
    all_to_all x1, blocking collectives, on_device(): lax.all_to_all(kv_send.reshape(32, 2, 128, 128), KEY_GROUP, 0, 0, tiled=T...  38.6 us
    all_to_all x1, blocking collectives, on_device(): lax.all_to_all(q_send.reshape(32, 64, 128), QUERY_GROUP, 0, 0, tiled=True)  30 us
    all_to_all x1, blocking collectives, on_device(): o_recv = lax.all_to_all(o_send, QUERY_GROUP, 0, 0, tiled=True)  24.6 us
    pallas_call x1, Pallas kernels, on_device(): pl.pallas_call(functools.partial(attend_kernel, True), out_shape=jax.Shap...  13.4 us
    pallas_call x1, Pallas kernels, on_device(): pl.pallas_call(functools.partial(attend_kernel, False), out_shape=(jax.Sh...  12.9 us
    ppermute x1, waiting for transfers between devices, on_device(): lax.ppermute(visual_keyval, AXES, [(i, i - 1) for i in range(1, owners)])  3.48 us
    unnamed x8, local copies, waits for them, and re-layouts  2.65 us
  transfers between devices with their start and end apart: 2, of which 1 were waited for; matrix products, arithmetic and copies ran while one was open for 0% of the time, Pallas kernels for 10%

profile of v1, /device:TPU:32, one launch (start us, length us, event | category | flops | bytes accessed | tf_op | source)
XLA Modules:
  0.0 129.3 jit_solution(11789468662441706921)
XLA Ops:
  0.0 1.9 %collective-permute-start = (bf16[48,8,2,128]{3,2,1,0:T(2,128)(2,1)}, bf16[48,8,2,128]{3,2,1,0:T(2,128)(2,1)S(1)}, u32[]{:S(2)}, u32[]{:S(2)}) collective-permute-start(bf16[48,8,2,128]{3,2,1,0:T(2,128)(2,1)} %param.6), channel_id=1, source_target_pairs={{1,0},{2,1},{3,2},{4,3},{5,4},{6,5},{7,6},{8,7},{9,8},{10,9},{11,1... | collective-permute-start | bytes 589832 | tf_op jit(solution)/shard_map/ppermute | solution.py:186
  1.9 3.5 %collective-permute-done = bf16[48,8,2,128]{3,2,1,0:T(2,128)(2,1)S(1)} collective-permute-done((bf16[48,8,2,128]{3,2,1,0:T(2,128)(2,1)}, bf16[48,8,2,128]{3,2,1,0:T(2,128)(2,1)S(1)}, u32[]{:S(2)}, u32[]{:S(2)}) %collective-permute-start) | collective-permute-done | bytes 196640 | tf_op jit(solution)/shard_map/ppermute | solution.py:186
  5.4 0.0 copy-start
  5.4 1.0 copy-done
  6.4 0.0 copy-start.1
  6.4 0.9 copy-done.1
  7.4 0.0 copy-start.3
  7.4 0.7 copy-done.3
  8.0 0.6 place_rows.1
  8.7 0.0 copy-start.2
  8.7 38.6 %all_to_all.15.refs_1_ = bf16[32,2,128,128]{3,2,1,0:T(8,128)(2,1)S(1)} all-to-all(bf16[32,2,128,128]{3,2,1,0:T(8,128)(2,1)S(1)} %bitcast.7), channel_id=1, replica_groups=mesh['x'=4,'zh'=2,'y'=4,'k'=2,'zp'=2,'c'=2] {'x','y','zp'}, dimensions={0} | all-to-all | bytes 4194304 | tf_op jit(solution)/shard_map/all_to_all | solution.py:211
  47.3 0.0 collective-permute-start.1
  47.3 0.0 copy-done.2
  47.3 0.1 query_chunks.1
  47.4 30.0 %all_to_all.16 = bf16[32,64,128]{2,1,0:T(8,128)(2,1)S(1)} all-to-all(bf16[32,64,128]{2,1,0:T(8,128)(2,1)S(1)} %bitcast.10), channel_id=1, replica_groups=mesh['x'=4,'zh'=2,'y'=4,'k'=2,'zp'=2,'c'=2] {'x','zh','k','zp'}, dimensions={0} | all-to-all | bytes 1048576 | tf_op jit(solution)/shard_map/all_to_all | solution.py:195
  77.4 12.9 %attend_first.1 = (f32[2048,256]{1,0:T(8,128)S(1)}, f32[2048,128]{1,0:T(8,128)S(1)}) custom-call(bf16[2048,128]{1,0:T(8,128)(2,1)S(1)} %bitcast.8, bf16[32,2,128,128]{3,2,1,0:T(8,128)(2,1)S(1)} %all_to_all.15.refs_1_), custom_call_target="tpu_custom_call" | custom-call | flops 5368709120 | bytes 6291456 | tf_op jit(solution)/shard_map/attend_first/pallas_call | solution.py:213
  90.2 0.0 collective-permute-done.1.refs_1_
  90.2 13.4 %attend_last.1 = bf16[32,80,128]{2,1,0:T(8,128)(2,1)S(1)} custom-call(bf16[2048,128]{1,0:T(8,128)(2,1)S(1)} %bitcast.9, bf16[32,2,128,128]{3,2,1,0:T(8,128)(2,1)S(1)} %collective-permute-done.1.refs_1_, f32[2048,256]{1,0:T(8,128)S(1)} %get-tuple-element.7.refs_2_, f32[2048,128]{1,0:T(8,128)S(1)} %get-tuple-element.8.refs_3_), custom_call_target="tpu_custom_call" | custom-call | tf_op jit(solution)/shard_map/attend_last/pallas_call | solution.py:227
  103.6 24.6 %all_to_all.17.recv_ref = bf16[32,80,128]{2,1,0:T(8,128)(2,1)S(1)} all-to-all(bf16[32,80,128]{2,1,0:T(8,128)(2,1)S(1)} %attend_last.1), channel_id=1, replica_groups=mesh['x'=4,'zh'=2,'y'=4,'k'=2,'zp'=2,'c'=2] {'x','zh','k','zp'}, dimensions={0} | all-to-all | bytes 1310720 | tf_op jit(solution)/shard_map/all_to_all | solution.py:235
  128.2 1.0 combine_parts.1
Async XLA Ops:
  0.0 5.4 %collective-permute-start = (bf16[48,8,2,128]{3,2,1,0:T(2,128)(2,1)}, bf16[48,8,2,128]{3,2,1,0:T(2,128)(2,1)S(1)}, u32[]{:S(2)}, u32[]{:S(2)}) collective-permute-start(bf16[48,8,2,128]{3,2,1,0:T(2,128)(2,1)} %param.6), channel_id=1, source_target_pairs={{1,0},{2,1},{3,2},{4,3},{5,4},{6,5},{7,6},{8,7},{9,8},{10,9},{11,1... | collective-permute-start | bytes 589832 | tf_op jit(solution)/shard_map/ppermute | solution.py:186
  5.4 1.0 copy-start
  6.4 0.9 copy-start.1
  7.4 0.7 copy-start.3
  8.7 38.6 %copy-start.2 = (bf16[8,64,128]{2,1,0:T(8,128)(2,1)S(1)}, bf16[8,64,128]{2,1,0:T(8,128)(2,1)}, u32[]{:S(2)}) copy-start(bf16[8,64,128]{2,1,0:T(8,128)(2,1)} %q_ref.1) | copy-start | bytes 393220
  47.3 42.9 %collective-permute-start.1 = (bf16[32,2,128,128]{3,2,1,0:T(8,128)(2,1)S(1)}, bf16[32,2,128,128]{3,2,1,0:T(8,128)(2,1)S(1)}, u32[]{:S(2)}, u32[]{:S(2)}) collective-permute-start(bf16[32,2,128,128]{3,2,1,0:T(8,128)(2,1)S(1)} %all_to_all.15.refs_1_), channel_id=1, source_target_pairs={{0,1},{1,0},{2,3},{3,2},{4,5},{5,4},{6,7},{7,6},{8,9},{9,8},{10,11... | collective-permute-start | bytes 6291464 | tf_op jit(solution)/shard_map/ppermute | solution.py:212

commit v2 on v1

v2 whole, which is shorter than its diff:
```python
import functools
import math

import jax
import jax.numpy as jnp
from jax import lax
from jax.experimental import pallas as pl
from jax.experimental.pallas import tpu as pltpu
from jax.sharding import Mesh, PartitionSpec as P

AXES = ("x", "zh", "y", "k", "zp", "c")
SIZES = (4, 2, 4, 2, 2, 2)
QUERY_GROUP = ("x", "zh", "k", "zp")
NEVER = -1e30
VMEM = pl.BlockSpec(memory_space=pltpu.VMEM)
SMEM = pl.BlockSpec(memory_space=pltpu.SMEM)


def head_order():
    out_row = lax.broadcasted_iota(jnp.int32, (256, 256), 0)
    in_row = lax.broadcasted_iota(jnp.int32, (256, 256), 1)
    moves = jnp.where(in_row == (out_row % 16) * 16 + out_row // 16, 1.0, 0.0)
    return moves.astype(jnp.bfloat16)


def local_kernel(
    counts_ref, q_ref, text_ref, vis_ref, q_out_ref, moved_ref, vis_out_ref, window_ref
):
    owner = 0
    for axis, size in zip(AXES, SIZES):
        owner = owner * size + lax.axis_index(axis)
    counts = counts_ref[...].astype(jnp.float32)
    order = lax.broadcasted_iota(jnp.int32, counts.shape, 0) * 128 + lax.broadcasted_iota(
        jnp.int32, counts.shape, 1
    )
    before = jnp.sum(jnp.where(order < owner, counts, 0.0)).astype(jnp.int32)
    here = jnp.sum(jnp.where(order == owner, counts, 0.0)).astype(jnp.int32)
    window_ref[0] = jnp.clip(before - owner * 48, 0, 47)
    window_ref[1] = here
    for pair in range(4):
        both = q_ref[:, pair * 16 : (pair + 1) * 16, :].astype(jnp.float32)
        for zp in range(2):
            chunk = both[:, zp * 8 : (zp + 1) * 8, :].reshape(64, 128)
            q_out_ref[pair * 2 + zp] = chunk.astype(jnp.bfloat16)
    vis_out_ref[...] = vis_ref[...]
    moves = head_order()
    for part in range(8):
        rows = slice(part * 256, (part + 1) * 256)
        moved_ref[rows] = jnp.dot(
            moves, text_ref[rows], preferred_element_type=jnp.float32
        ).astype(jnp.bfloat16)


def scale_kernel(mine_ref, near_ref, across_ref, far_ref, out_ref):
    scale = math.log2(math.e) / math.sqrt(128)
    for xq in range(4):
        rows = slice(xq * 128, (xq + 1) * 128)
        sets = [ref[rows] for ref in (mine_ref, near_ref, across_ref, far_ref)]
        scaled = jnp.concatenate(sets, axis=0).astype(jnp.float32) * scale
        high = scaled.astype(jnp.bfloat16)
        low = (scaled - high.astype(jnp.float32)).astype(jnp.bfloat16)
        out_ref[xq * 512 : (xq + 1) * 512] = jnp.concatenate([high, low], axis=1)


def place_kernel(window_ref, q_ref, moved_ref, vis_ref, next_ref, send_ref, stacked):
    send_ref[:, 256:320] = q_ref[...]
    start = window_ref[0]
    here = window_ref[1]
    stacked[0:768] = vis_ref[...]
    stacked[768:1536] = next_ref[...]
    stacked[1536:2304] = jnp.zeros((768, 128), jnp.bfloat16)
    moves = head_order()
    row_within = lax.broadcasted_iota(jnp.int32, (256, 128), 0) % 16
    for part in range(8):
        data = moved_ref[part * 256 : (part + 1) * 256]
        if part < 6:
            first = pl.multiple_of(start * 16 + part * 256, 16)
            window = jnp.dot(moves, stacked[pl.ds(first, 256)], preferred_element_type=jnp.float32)
            data = jnp.where(row_within + part * 16 < here, window, data.astype(jnp.float32))
            data = data.astype(jnp.bfloat16)
        for head in range(8):
            for kind in range(2):
                slab = data[(head * 2 + kind) * 16 : (head * 2 + kind + 1) * 16]
                first_row = kind * 128 + part * 16
                send_ref[head, first_row : first_row + 16] = slab


ROWS = 512


def attend_kernel(steps, swapped, shared, first, last, q_ref, *refs):
    refs = list(refs)
    kv_refs = [refs.pop(0) for _ in range(1 if shared else 2)]
    if shared:
        kv_refs = [kv_refs[0].at[0:8], kv_refs[0].at[8:16]]
    if not first:
        acc_in, m_in = refs[:2]
        refs = refs[2:]
    if last:
        (send_ref,) = refs
    else:
        acc_ref, m_ref = refs
    me = {axis: lax.axis_index(axis) for axis in ("zh", "y", "k", "c")}
    width = 512
    y = (me["y"] + steps[0] + steps[1] * me["c"]) % 4
    ones = jnp.ones((width, 128), jnp.bfloat16)
    row = lax.broadcasted_iota(jnp.int32, (ROWS, 128), 0)
    lane = lax.broadcasted_iota(jnp.int32, (ROWS, 128), 1)
    pair = me["zh"] * 2 + me["k"]
    turns = (0, 3 - 2 * me["c"], 2, 1 + 2 * me["c"])
    turn = functools.reduce(
        lambda so_far, j: jnp.where(row // 128 == j, turns[j], so_far), range(1, 4), row * 0
    )
    z = (pair + turn) % 4
    q_dev = (z // 2) * 32 + me["y"] * 8 + (z % 2) * 4 + (row // 64 % 2) * 2 + me["c"]
    reach = q_dev * 128 + 120 + (row % 64) // 8 - lane
    queries, state = {}, {}
    for xq in range(4):
        rows = slice(xq * ROWS, (xq + 1) * ROWS)
        queries[xq] = q_ref[rows]
        state[xq] = None if first else (m_in[rows], acc_in[rows])

    def gathered(xk, kind):
        found = []
        for kv_ref in kv_refs:
            rows = kv_ref[xk * 2 : xk * 2 + 2, kind * 128 : (kind + 1) * 128]
            found.append(rows.reshape(256, 128))
        return jnp.concatenate(found, axis=0)

    def score(xq, xk):
        keys = gathered(xk, 0)
        return lax.dot_general(
            queries[xq],
            jnp.concatenate([keys, keys], axis=1),
            (((1,), (1,)), ((), ())),
            preferred_element_type=jnp.float32,
        )

    def absorb(xq, xk, scores):
        parts = [scores[:, j * 128 : (j + 1) * 128] for j in range(width // 128)]
        if xk == xq:
            for j in range(width // 128):
                core = me["c"] if j // 2 == swapped else 1 - me["c"]
                k_dev = me["zh"] * 32 + y * 8 + me["k"] * 4 + j % 2 * 2 + core
                parts[j] = jnp.where(reach >= k_dev * 128, parts[j], NEVER)
        top = jnp.max(functools.reduce(jnp.maximum, parts), axis=1, keepdims=True)
        if state[xq] is None:
            new = jnp.broadcast_to(top, (ROWS, 128))
        else:
            new = jnp.maximum(state[xq][0], top)
        weights = jnp.concatenate(
            [jnp.exp2(part - new).astype(jnp.bfloat16) for part in parts], axis=1
        )
        values = gathered(xk, 1)
        acc = jnp.dot(
            weights, jnp.concatenate([values, ones], axis=1), preferred_element_type=jnp.float32
        )
        if state[xq] is not None:
            shrink = jnp.exp2(state[xq][0] - new)
            acc = state[xq][1] * jnp.concatenate([shrink, shrink], axis=1) + acc
        state[xq] = (new, acc)

    def finish(xq):
        maxima, acc = state[xq]
        if not last:
            m_ref[xq * ROWS : (xq + 1) * ROWS] = maxima
            acc_ref[xq * ROWS : (xq + 1) * ROWS] = acc
            return
        totals = acc[:, 128:]
        result = (acc[:, :128] / totals).astype(jnp.bfloat16)
        level = maxima + jnp.log2(totals)
        eye = lax.broadcasted_iota(jnp.int32, (64, 128), 0) == lax.broadcasted_iota(
            jnp.int32, (64, 128), 1
        )
        stat_row = lax.broadcasted_iota(jnp.int32, (16, 128), 0)
        for j in range(8):
            chunk = xq * 8 + (pair + turns[j // 2]) % 4 * 2 + j % 2
            send_ref[chunk, :64] = result[j * 64 : (j + 1) * 64]
            line = jnp.where(eye, level[j * 64 : (j + 1) * 64], 0.0)
            line = jnp.sum(line, axis=0, keepdims=True)
            one = line.astype(jnp.bfloat16).astype(jnp.float32)
            two = (line - one).astype(jnp.bfloat16).astype(jnp.float32)
            three = line - one - two
            stats = jnp.where(stat_row == 2, three, 0.0)
            stats = jnp.where(stat_row == 0, one, jnp.where(stat_row == 1, two, stats))
            send_ref[chunk, 64:80] = stats.astype(jnp.bfloat16)

    order = [(3, 0), (2, 0), (1, 0), (0, 0), (3, 1), (2, 1), (1, 1), (3, 2), (2, 2), (3, 3)]
    scores = score(*order[0])
    for now, later in zip(order, order[1:] + [None]):
        ahead = None if later is None else score(*later)
        absorb(*now, scores)
        if now[0] == now[1]:
            finish(now[0])
        scores = ahead


def combine_kernel(recv_ref, out_ref):
    eye = lax.broadcasted_iota(jnp.int32, (64, 128), 0) == lax.broadcasted_iota(
        jnp.int32, (64, 128), 1
    )
    for x in range(4):
        heads = []
        for zp in range(2):
            chunks = [x * 8 + part * 2 + zp for part in range(4)]
            levels = []
            for chunk in chunks:
                stats = recv_ref[chunk, 64:80].astype(jnp.float32)
                levels.append(stats[0:1] + stats[1:2] + stats[2:3])
            top = functools.reduce(jnp.maximum, levels)
            shares = [jnp.exp2(level - top) for level in levels]
            whole = functools.reduce(jnp.add, shares)
            total = None
            for chunk, share in zip(chunks, shares):
                column = jnp.sum(jnp.where(eye, share / whole, 0.0), axis=1, keepdims=True)
                term = recv_ref[chunk, :64].astype(jnp.float32) * column
                total = term if total is None else total + term
            heads.append(total.reshape(8, 8, 128))
        out_ref[:, x * 16 : (x + 1) * 16, :] = jnp.concatenate(heads, axis=1).astype(jnp.bfloat16)


def params():
    return pltpu.CompilerParams(vmem_limit_bytes=40 * 1024 * 1024)


def cost(flops, exps, size):
    return pl.CostEstimate(flops=flops, bytes_accessed=size, transcendentals=exps)


def on_device(queries, text_keyval, visual_keyval, visual_counts):
    owners = math.prod(SIZES)
    following = lax.ppermute(visual_keyval, AXES, [(i, i - 1) for i in range(1, owners)])
    q_chunks, moved, visual, window = pl.pallas_call(
        local_kernel,
        out_shape=(
            jax.ShapeDtypeStruct((8, 64, 128), jnp.bfloat16),
            jax.ShapeDtypeStruct((2048, 128), jnp.bfloat16),
            jax.ShapeDtypeStruct((768, 128), jnp.bfloat16),
            jax.ShapeDtypeStruct((2,), jnp.int32),
        ),
        in_specs=[VMEM] * 4,
        out_specs=(VMEM, VMEM, VMEM, SMEM),
        compiler_params=params(),
        cost_estimate=cost(2 * 2048 * 256 * 128, 0, 3 * 2**20),
        name="local_rows",
    )(
        visual_counts.reshape(2, 128),
        queries,
        text_keyval.reshape(2048, 128),
        visual_keyval.reshape(768, 128),
    )
    send = pl.pallas_call(
        place_kernel,
        out_shape=jax.ShapeDtypeStruct((8, 320, 128), jnp.bfloat16),
        in_specs=[SMEM, VMEM, VMEM, VMEM, VMEM],
        out_specs=VMEM,
        scratch_shapes=[pltpu.VMEM((48 * 3 * 16, 128), jnp.bfloat16)],
        compiler_params=params(),
        cost_estimate=cost(2 * 1536 * 256 * 128, 0, 2**21),
        name="place_rows",
    )(window, q_chunks, moved, visual, following.reshape(768, 128))
    received = lax.all_to_all(send, ("x", "zp"), 0, 0, tiled=True)
    kv = received[:, :256]
    q_mine = received[:, 256:].reshape(512, 128)

    def apart(value, axis):
        turns = [(2 * i + c, 2 * ((i + 1 - 2 * c) % 4) + c) for i in range(4) for c in range(2)]
        return lax.ppermute(value, (*axis, "c"), turns)

    def swap(value):
        return lax.ppermute(value, "c", [(0, 1), (1, 0)])

    q_pair = apart(jnp.concatenate([q_mine, swap(q_mine)], axis=0), ("zh", "k"))
    q_near = q_pair[:512]
    q_far = swap(q_pair[512:])
    q_across = apart(q_near, ("zh", "k"))
    kv_own = jnp.concatenate([kv, swap(kv)], axis=0)
    kv_near = apart(kv_own, ("y",))
    kv_far = swap(kv_near)
    kv_across = apart(kv_near[:8], ("y",))
    q_all = pl.pallas_call(
        scale_kernel,
        out_shape=jax.ShapeDtypeStruct((2048, 256), jnp.bfloat16),
        in_specs=[VMEM] * 4,
        out_specs=VMEM,
        compiler_params=params(),
        cost_estimate=cost(2**20, 0, 2**21),
        name="scale_queries",
    )(q_mine, q_near, q_across, q_far)

    def attend(name, steps, swapped, values, state, weight=4):
        last = name == "attend_d"
        if last:
            out_shape, out_specs = jax.ShapeDtypeStruct((32, 80, 128), jnp.bfloat16), VMEM
        else:
            out_shape = (
                jax.ShapeDtypeStruct((2048, 256), jnp.float32),
                jax.ShapeDtypeStruct((2048, 128), jnp.float32),
            )
            out_specs = (VMEM, VMEM)
        operands = (q_all, *values, *state)
        return pl.pallas_call(
            functools.partial(
                attend_kernel, steps, swapped, len(values) == 1, not state, last
            ),
            out_shape=out_shape,
            in_specs=[VMEM] * len(operands),
            out_specs=out_specs,
            compiler_params=params(),
            cost_estimate=cost(weight * 2621440 * 256, 2621440, 6 * 2**20),
            name=name,
        )(*operands)

    state = attend("attend_a", (0, 0), 0, (kv_own,), ())
    state = attend("attend_b", (3, -2), 0, (kv_near,), state)
    state = attend("attend_c", (1, 2), 1, (kv_far,), state, 16)
    o_send = attend("attend_d", (2, 0), 0, (kv_across, swap(kv_across)), state)
    o_recv = lax.all_to_all(o_send, QUERY_GROUP, 0, 0, tiled=True)
    return pl.pallas_call(
        combine_kernel,
        out_shape=jax.ShapeDtypeStruct((8, 64, 128), jnp.bfloat16),
        in_specs=[VMEM],
        out_specs=VMEM,
        compiler_params=params(),
        cost_estimate=cost(2**20, 4096, 2**20),
        name="combine_parts",
    )(o_recv)


def solution(mesh):
    fine = Mesh(mesh.devices.reshape(SIZES), AXES)
    in_specs = (
        P(AXES, None, None),
        P(AXES, None, None, None),
        P(AXES, None, None, None),
        P(),
    )
    out_specs = P(AXES, None, None)
    return jax.shard_map(
        on_device, mesh=fine, in_specs=in_specs, out_specs=out_specs, check_vma=False
    )
```

time: 130 us -> 96.8 us (0.74)
  blocking collectives: 93.2 us -> 47.6 us
  waiting for transfers between devices: 3.48 us -> 18.8 us
  Pallas kernels: 28 us -> 17.5 us
  starting transfers between devices: 1.91 us -> 8.6 us
    all_to_all x2 -> x1, blocking collectives: 68.6 us -> 20.2 us  [on_device(): received = lax.all_to_all(send, ('x', 'zp'), 0, 0, tiled=True)]
    ppermute x1 -> x9, waiting for transfers between devices: 0.01 us -> 18.8 us  [the longest x4 15.7 us: apart(): return lax.ppermute(value, (*axis, 'c'), turns)]
    pallas_call x4 -> x7, Pallas kernels: 26.9 us -> 16.5 us  [the longest x4 14.3 us: attend(): pl.pallas_call(functools.partial(attend_kernel, steps, swapped, len(value...]
    ppermute x1 -> x9, starting transfers between devices: 0.01 us -> 6.7 us  [the longest x4 3.44 us: apart(): return lax.ppermute(value, (*axis, 'c'), turns)]
    ppermute x1, waiting for transfers between devices: 3.48 us -> 0.01 us  [on_device(): lax.ppermute(visual_keyval, AXES, [(i, i - 1) for i in range(1, owners)])]
    all_to_all x1, blocking collectives: 24.6 us -> 27.5 us  [on_device(): o_recv = lax.all_to_all(o_send, QUERY_GROUP, 0, 0, tiled=True)]
  transfers between devices with their start and end apart: 2 -> 10, of which waited for: 1 -> 4; matrix products, arithmetic and copies ran while one was open for 0% -> 0% of each run, Pallas kernels for 10% -> 12%
where the time goes in v2:
time: 96.8 us; the launch traced here: 96.5 us
  blocking collectives  47.6 us (49%)
  waiting for transfers between devices  18.8 us (19%)
  Pallas kernels  17.5 us (18%)
  starting transfers between devices  8.6 us (9%)
  local copies, waits for them, and re-layouts  3.64 us (4%)
    all_to_all x1, blocking collectives, on_device(): o_recv = lax.all_to_all(o_send, QUERY_GROUP, 0, 0, tiled=True)  27.5 us
    all_to_all x1, blocking collectives, on_device(): received = lax.all_to_all(send, ('x', 'zp'), 0, 0, tiled=True)  20.2 us
    ppermute x4, waiting for transfers between devices, apart(): return lax.ppermute(value, (*axis, 'c'), turns)  15.7 us
    pallas_call x4, Pallas kernels, attend(): pl.pallas_call(functools.partial(attend_kernel, steps, swapped, len(value...  14.3 us
    unnamed x8, local copies, waits for them, and re-layouts  3.54 us
    ppermute x4, starting transfers between devices, apart(): return lax.ppermute(value, (*axis, 'c'), turns)  3.44 us
    ppermute x5, starting transfers between devices, swap(): return lax.ppermute(value, 'c', [(0, 1), (1, 0)])  3.26 us
    ppermute x5, waiting for transfers between devices, swap(): return lax.ppermute(value, 'c', [(0, 1), (1, 0)])  3.12 us
  transfers between devices with their start and end apart: 10, of which 4 were waited for; matrix products, arithmetic and copies ran while one was open for 0% of the time, Pallas kernels for 12%

profile of v2, /device:TPU:32, one launch (start us, length us, event | category | flops | bytes accessed | tf_op | source)
XLA Modules:
  0.0 96.5 jit_solution(57379387752340684)
XLA Ops:
  0.0 1.9 %collective-permute-start = (bf16[48,8,2,128]{3,2,1,0:T(2,128)(2,1)}, bf16[48,8,2,128]{3,2,1,0:T(2,128)(2,1)S(1)}, u32[]{:S(2)}, u32[]{:S(2)}) collective-permute-start(bf16[48,8,2,128]{3,2,1,0:T(2,128)(2,1)} %param.6), channel_id=1, source_target_pairs={{1,0},{2,1},{3,2},{4,3},{5,4},{6,5},{7,6},{8,7},{9,8},{10,9},{11,1... | collective-permute-start | bytes 589832 | tf_op jit(solution)/shard_map/ppermute | solution.py:232
  1.9 1.0 %copy-done = bf16[128,8,2,128]{3,2,1,0:T(2,128)(2,1)S(1)} copy-done((bf16[128,8,2,128]{3,2,1,0:T(2,128)(2,1)S(1)}, bf16[128,8,2,128]{3,2,1,0:T(2,128)(2,1)}, u32[]{:S(2)}) %copy-start) | copy-done | bytes 524312
  3.0 0.9 copy-done.1
  3.9 0.9 copy-done.2
  4.8 0.7 copy-done.3
  5.5 1.0 %local_rows.1 = (bf16[8,64,128]{2,1,0:T(8,128)(2,1)S(1)}, bf16[2048,128]{1,0:T(8,128)(2,1)S(1)}, bf16[768,128]{1,0:T(8,128)(2,1)S(1)}, s32[2]{0:T(128)S(1)}) custom-call(s32[2,128]{1,0:T(2,128)S(1)} %bitcast.11, bf16[8,64,128]{2,1,0:T(8,128)(2,1)S(1)} %copy-done.2, bf16[2048,128]{1,0:T(8,128)(2,1)S(1)} %bitcast.8, bf16[768,128]{1,0:T(8,128)(2,1)S(1)} %bitcast.10), custom_call_target="tpu_custom_call" | custom-call | flops 134217728 | bytes 3145728 | tf_op jit(solution)/shard_map/local_rows/pallas_call | solution.py:233
  6.5 0.0 collective-permute-done
  6.5 1.0 place_rows.1
  7.5 20.2 %all_to_all.10 = bf16[8,320,128]{2,1,0:T(8,128)(2,1)S(1)} all-to-all(bf16[8,320,128]{2,1,0:T(8,128)(2,1)S(1)} %place_rows.1), channel_id=1, replica_groups=mesh['x'=4,'zh'=2,'y'=4,'k'=2,'zp'=2,'c'=2] {'x','zp'}, dimensions={0} | all-to-all | bytes 1310720 | tf_op jit(solution)/shard_map/all_to_all | solution.py:262
  27.7 0.1 collective-permute-start.5
  27.8 1.9 %collective-permute-done.5 = bf16[8,256,128]{2,1,0:T(8,128)(2,1)S(1)} collective-permute-done((bf16[8,256,128]{2,1,0:T(8,128)(2,1)S(1)}, bf16[8,256,128]{2,1,0:T(8,128)(2,1)S(1)}, u32[]{:S(2)}, u32[]{:S(2)}) %collective-permute-start.5) | collective-permute-done | bytes 524320 | tf_op jit(solution)/shard_map/ppermute | solution.py:271
  29.6 0.1 pad_maximum_fusion.refs_0_
  29.7 0.1 collective-permute-start.6
  29.9 0.2 collective-permute-start.1
  30.1 1.2 %collective-permute-done.1 = bf16[512,128]{1,0:T(8,128)(2,1)S(1)} collective-permute-done((bf16[512,128]{1,0:T(8,128)(2,1)S(1)}, bf16[512,128]{1,0:T(8,128)(2,1)S(1)}, u32[]{:S(2)}, u32[]{:S(2)}) %collective-permute-start.1) | collective-permute-done | bytes 131104 | tf_op jit(solution)/shard_map/ppermute | solution.py:271
  31.3 2.6 %collective-permute-start.2 = (bf16[1024,128]{1,0:T(8,128)(2,1)S(1)}, bf16[1024,128]{1,0:T(8,128)(2,1)S(1)}, u32[]{:S(2)}, u32[]{:S(2)}) collective-permute-start(bf16[1024,128]{1,0:T(8,128)(2,1)S(1)} %pad_maximum_fusion.1), channel_id=1, source_target_pairs={{0,4},{1,37},{4,32},{5,1},{32,36},{33,5},{36,0},{37,33},{2,6},{3,3... | collective-permute-start | bytes 786440 | tf_op jit(solution)/shard_map/ppermute | solution.py:268
  34.0 11.9 %collective-permute-done.6.refs_0_ = bf16[16,256,128]{2,1,0:T(8,128)(2,1)S(1)} collective-permute-done((bf16[16,256,128]{2,1,0:T(8,128)(2,1)S(1)}, bf16[16,256,128]{2,1,0:T(8,128)(2,1)S(1)}, u32[]{:S(2)}, u32[]{:S(2)}) %collective-permute-start.6) | collective-permute-done | bytes 1048608 | tf_op jit(solution)/shard_map/ppermute | solution.py:268
  45.8 0.0 collective-permute-start.9
  45.8 0.0 collective-permute-done.2
  45.9 0.1 collective-permute-start.3
  46.0 2.6 %collective-permute-start.4 = (bf16[512,128]{1,0:T(8,128)(2,1)S(1)}, bf16[512,128]{1,0:T(8,128)(2,1)S(1)}, u32[]{:S(2)}, u32[]{:S(2)}) collective-permute-start(bf16[512,128]{1,0:T(8,128)(2,1)S(1)} %get-tuple-element.25), channel_id=1, source_target_pairs={{0,1},{1,0},{2,3},{3,2},{4,5},{5,4},{6,7},{7,6},{8,9},{9,8},{10,11... | collective-permute-start | bytes 393224 | tf_op jit(solution)/shard_map/ppermute | solution.py:271
  48.6 0.6 collective-permute-start.7
  49.2 3.8 %collective-permute-done.3.across_ref = bf16[512,128]{1,0:T(8,128)(2,1)S(1)} collective-permute-done((bf16[512,128]{1,0:T(8,128)(2,1)S(1)}, bf16[512,128]{1,0:T(8,128)(2,1)S(1)}, u32[]{:S(2)}, u32[]{:S(2)}) %collective-permute-start.3) | collective-permute-done | bytes 131104 | tf_op jit(solution)/shard_map/ppermute | solution.py:268
  53.1 0.2 scale_queries.1.q_ref
  53.3 3.5 %attend_a.1 = (f32[2048,256]{1,0:T(8,128)S(1)}, f32[2048,128]{1,0:T(8,128)S(1)}) custom-call(bf16[2048,256]{1,0:T(8,128)(2,1)S(1)} %scale_queries.1.q_ref, bf16[16,256,128]{2,1,0:T(8,128)(2,1)S(1)} %pad_maximum_fusion.refs_0_), custom_call_target="tpu_custom_call" | custom-call | flops 2684354560 | bytes 6291456 | tf_op jit(solution)/shard_map/attend_a/pallas_call | solution.py:302
  56.7 3.6 %attend_b.1 = (f32[2048,256]{1,0:T(8,128)S(1)}, f32[2048,128]{1,0:T(8,128)S(1)}) custom-call(bf16[2048,256]{1,0:T(8,128)(2,1)S(1)} %scale_queries.1.q_ref, bf16[16,256,128]{2,1,0:T(8,128)(2,1)S(1)} %collective-permute-done.6.refs_0_, f32[2048,256]{1,0:T(8,128)S(1)} %get-tuple-element.19.refs_1_, f32[2048,128]{1,0:T(8,128)S(1)} %get-tuple-element.20.refs_2_), custom_call_target="tpu_custom_call" | custom-call | flops 2684354560 | bytes 6291456 | tf_op jit(solution)/shard_map/attend_b/pallas_call | solution.py:302
  60.3 0.3 collective-permute-start.8
  60.7 3.6 %attend_c.1 = (f32[2048,256]{1,0:T(8,128)S(1)}, f32[2048,128]{1,0:T(8,128)S(1)}) custom-call(bf16[2048,256]{1,0:T(8,128)(2,1)S(1)} %scale_queries.1.q_ref, bf16[16,256,128]{2,1,0:T(8,128)(2,1)S(1)} %collective-permute-done.9.refs_0_, f32[2048,256]{1,0:T(8,128)S(1)} %get-tuple-element.21.refs_1_, f32[2048,128]{1,0:T(8,128)S(1)} %get-tuple-element.22.refs_2_), custom_call_target="tpu_custom_call" | custom-call | flops 10737418240 | bytes 6291456 | tf_op jit(solution)/shard_map/attend_c/pallas_call | solution.py:302
  64.2 0.0 collective-permute-done.8.refs_1_
  64.3 3.8 %attend_d.1 = bf16[32,80,128]{2,1,0:T(8,128)(2,1)S(1)} custom-call(bf16[2048,256]{1,0:T(8,128)(2,1)S(1)} %scale_queries.1.q_ref, bf16[8,256,128]{2,1,0:T(8,128)(2,1)S(1)} %collective-permute-done.7.refs_0_, bf16[8,256,128]{2,1,0:T(8,128)(2,1)S(1)} %collective-permute-done.8.refs_1_, f32[2048,256]{1,0:T(8,128)S(1)} %get-tuple-element.23.refs_2_, ...), custom_call_target="tpu_custom_call" | custom-call | flops 2684354560 | bytes 6291456 | tf_op jit(solution)/shard_map/attend_d/pallas_call | solution.py:302
  68.0 27.5 %all_to_all.11.recv_ref = bf16[32,80,128]{2,1,0:T(8,128)(2,1)S(1)} all-to-all(bf16[32,80,128]{2,1,0:T(8,128)(2,1)S(1)} %attend_d.1), channel_id=1, replica_groups=mesh['x'=4,'zh'=2,'y'=4,'k'=2,'zp'=2,'c'=2] {'x','zh','k','zp'}, dimensions={0} | all-to-all | bytes 1310720 | tf_op jit(solution)/shard_map/all_to_all | solution.py:318
  95.5 1.0 %combine_parts.1 = bf16[8,64,128]{2,1,0:T(8,128)(2,1)} custom-call(bf16[32,80,128]{2,1,0:T(8,128)(2,1)S(1)} %all_to_all.11.recv_ref), custom_call_target="tpu_custom_call" | custom-call | flops 1048576 | bytes 1048576 | tf_op jit(solution)/shard_map/combine_parts/pallas_call | solution.py:319
  (12 shorter events, 0.1 us)
Async XLA Ops:
  0.0 6.5 %collective-permute-start = (bf16[48,8,2,128]{3,2,1,0:T(2,128)(2,1)}, bf16[48,8,2,128]{3,2,1,0:T(2,128)(2,1)S(1)}, u32[]{:S(2)}, u32[]{:S(2)}) collective-permute-start(bf16[48,8,2,128]{3,2,1,0:T(2,128)(2,1)} %param.6), channel_id=1, source_target_pairs={{1,0},{2,1},{3,2},{4,3},{5,4},{6,5},{7,6},{8,7},{9,8},{10,9},{11,1... | collective-permute-start | bytes 589832 | tf_op jit(solution)/shard_map/ppermute | solution.py:232
  1.9 1.0 %copy-start = (bf16[128,8,2,128]{3,2,1,0:T(2,128)(2,1)S(1)}, bf16[128,8,2,128]{3,2,1,0:T(2,128)(2,1)}, u32[]{:S(2)}) copy-start(bf16[128,8,2,128]{3,2,1,0:T(2,128)(2,1)} %param.5) | copy-start | bytes 1572868
  3.0 0.9 copy-start.1
  3.9 0.9 copy-start.2
  4.8 0.7 copy-start.3
  27.7 2.0 %collective-permute-start.5 = (bf16[8,256,128]{2,1,0:T(8,128)(2,1)S(1)}, bf16[8,256,128]{2,1,0:T(8,128)(2,1)S(1)}, u32[]{:S(2)}, u32[]{:S(2)}) collective-permute-start(bf16[8,256,128]{2,1,0:T(8,128)(2,1)S(1)} %slice.23), channel_id=1, source_target_pairs={{0,1},{1,0},{2,3},{3,2},{4,5},{5,4},{6,7},{7,6},{8,9},{9,8},{10,11... | collective-permute-start | bytes 1572872 | tf_op jit(solution)/shard_map/ppermute | solution.py:271
  29.7 16.1 %collective-permute-start.6 = (bf16[16,256,128]{2,1,0:T(8,128)(2,1)S(1)}, bf16[16,256,128]{2,1,0:T(8,128)(2,1)S(1)}, u32[]{:S(2)}, u32[]{:S(2)}) collective-permute-start(bf16[16,256,128]{2,1,0:T(8,128)(2,1)S(1)} %pad_maximum_fusion.refs_0_), channel_id=1, source_target_pairs={{0,8},{1,25},{8,16},{9,1},{16,24},{17,9},{24,0},{25,17},{2,10},{3,... | collective-permute-start | bytes 3145736 | tf_op jit(solution)/shard_map/ppermute | solution.py:268
  29.9 1.4 %collective-permute-start.1 = (bf16[512,128]{1,0:T(8,128)(2,1)S(1)}, bf16[512,128]{1,0:T(8,128)(2,1)S(1)}, u32[]{:S(2)}, u32[]{:S(2)}) collective-permute-start(bf16[512,128]{1,0:T(8,128)(2,1)S(1)} %bitcast.5), channel_id=1, source_target_pairs={{0,1},{1,0},{2,3},{3,2},{4,5},{5,4},{6,7},{7,6},{8,9},{9,8},{10,11... | collective-permute-start | bytes 393224 | tf_op jit(solution)/shard_map/ppermute | solution.py:271
  31.3 14.5 %collective-permute-start.2 = (bf16[1024,128]{1,0:T(8,128)(2,1)S(1)}, bf16[1024,128]{1,0:T(8,128)(2,1)S(1)}, u32[]{:S(2)}, u32[]{:S(2)}) collective-permute-start(bf16[1024,128]{1,0:T(8,128)(2,1)S(1)} %pad_maximum_fusion.1), channel_id=1, source_target_pairs={{0,4},{1,37},{4,32},{5,1},{32,36},{33,5},{36,0},{37,33},{2,6},{3,3... | collective-permute-start | bytes 786440 | tf_op jit(solution)/shard_map/ppermute | solution.py:268
  45.8 14.8 %collective-permute-start.9 = (bf16[16,256,128]{2,1,0:T(8,128)(2,1)S(1)}, bf16[16,256,128]{2,1,0:T(8,128)(2,1)S(1)}, u32[]{:S(2)}, u32[]{:S(2)}) collective-permute-start(bf16[16,256,128]{2,1,0:T(8,128)(2,1)S(1)} %collective-permute-done.6.refs_0_), channel_id=1, source_target_pairs={{0,1},{1,0},{2,3},{3,2},{4,5},{5,4},{6,7},{7,6},{8,9},{9,8},{10,11... | collective-permute-start | bytes 3145736 | tf_op jit(solution)/shard_map/ppermute | solution.py:271
  45.9 7.2 %collective-permute-start.3 = (bf16[512,128]{1,0:T(8,128)(2,1)S(1)}, bf16[512,128]{1,0:T(8,128)(2,1)S(1)}, u32[]{:S(2)}, u32[]{:S(2)}) collective-permute-start(bf16[512,128]{1,0:T(8,128)(2,1)S(1)} %get-tuple-element.26.near_ref), channel_id=1, source_target_pairs={{0,4},{1,37},{4,32},{5,1},{32,36},{33,5},{36,0},{37,33},{2,6},{3,3... | collective-permute-start | bytes 393224 | tf_op jit(solution)/shard_map/ppermute | solution.py:268
  46.0 7.1 %collective-permute-start.4 = (bf16[512,128]{1,0:T(8,128)(2,1)S(1)}, bf16[512,128]{1,0:T(8,128)(2,1)S(1)}, u32[]{:S(2)}, u32[]{:S(2)}) collective-permute-start(bf16[512,128]{1,0:T(8,128)(2,1)S(1)} %get-tuple-element.25), channel_id=1, source_target_pairs={{0,1},{1,0},{2,3},{3,2},{4,5},{5,4},{6,7},{7,6},{8,9},{9,8},{10,11... | collective-permute-start | bytes 393224 | tf_op jit(solution)/shard_map/ppermute | solution.py:271
  48.6 11.7 %collective-permute-start.7 = (bf16[8,256,128]{2,1,0:T(8,128)(2,1)S(1)}, bf16[8,256,128]{2,1,0:T(8,128)(2,1)S(1)}, u32[]{:S(2)}, u32[]{:S(2)}) collective-permute-start(bf16[8,256,128]{2,1,0:T(8,128)(2,1)S(1)} %slice.24), channel_id=1, source_target_pairs={{0,8},{1,25},{8,16},{9,1},{16,24},{17,9},{24,0},{25,17},{2,10},{3,... | collective-permute-start | bytes 1572872 | tf_op jit(solution)/shard_map/ppermute | solution.py:268
  60.3 3.9 %collective-permute-start.8 = (bf16[8,256,128]{2,1,0:T(8,128)(2,1)S(1)}, bf16[8,256,128]{2,1,0:T(8,128)(2,1)S(1)}, u32[]{:S(2)}, u32[]{:S(2)}) collective-permute-start(bf16[8,256,128]{2,1,0:T(8,128)(2,1)S(1)} %collective-permute-done.7.refs_0_), channel_id=1, source_target_pairs={{0,1},{1,0},{2,3},{3,2},{4,5},{5,4},{6,7},{7,6},{8,9},{9,8},{10,11... | collective-permute-start | bytes 1572872 | tf_op jit(solution)/shard_map/ppermute | solution.py:271

commit v3 on v2

--- a/solution.py
+++ b/solution.py
@@ -51,15 +51,16 @@
         ).astype(jnp.bfloat16)
 
 
-def scale_kernel(mine_ref, near_ref, across_ref, far_ref, out_ref):
+def scale_kernel(*refs):
+    *q_refs, out_ref = refs
     scale = math.log2(math.e) / math.sqrt(128)
+    size = 128 * len(q_refs)
     for xq in range(4):
-        rows = slice(xq * 128, (xq + 1) * 128)
-        sets = [ref[rows] for ref in (mine_ref, near_ref, across_ref, far_ref)]
+        sets = [ref[xq * 128 : (xq + 1) * 128] for ref in q_refs]
         scaled = jnp.concatenate(sets, axis=0).astype(jnp.float32) * scale
         high = scaled.astype(jnp.bfloat16)
         low = (scaled - high.astype(jnp.float32)).astype(jnp.bfloat16)
-        out_ref[xq * 512 : (xq + 1) * 512] = jnp.concatenate([high, low], axis=1)
+        out_ref[xq * size : (xq + 1) * size] = jnp.concatenate([high, low], axis=1)
 
 
 def place_kernel(window_ref, q_ref, moved_ref, vis_ref, next_ref, send_ref, stacked):
@@ -85,86 +86,110 @@
                 send_ref[head, first_row : first_row + 16] = slab
 
 
-ROWS = 512
-
-
-def attend_kernel(steps, swapped, shared, first, last, q_ref, *refs):
+FIRST_SET = (0, 1, 2)
+SECOND_SET = (3,)
+ONE_BY_ONE = [
+    ((xq,), xk)
+    for xq, xk in ((3, 0), (2, 0), (1, 0), (0, 0), (3, 1), (2, 1), (1, 1), (3, 2), (2, 2), (3, 3))
+]
+STACKED = [((0, 1, 2, 3), 0), ((1, 2, 3), 1), ((2, 3), 2), ((3,), 3)]
+
+
+def attend_kernel(sets, sources, first, last, *refs):
     refs = list(refs)
-    kv_refs = [refs.pop(0) for _ in range(1 if shared else 2)]
-    if shared:
-        kv_refs = [kv_refs[0].at[0:8], kv_refs[0].at[8:16]]
-    if not first:
-        acc_in, m_in = refs[:2]
-        refs = refs[2:]
+    q_refs = [refs.pop(0) for _ in sets]
+    kv_refs = []
+    for _, _, shared in sources:
+        ref = refs.pop(0)
+        kv_refs.append([ref.at[0:8], ref.at[8:16]] if shared else [ref, refs.pop(0)])
+    states_in = [] if first else [(refs.pop(0), refs.pop(0)) for _ in sets]
     if last:
         (send_ref,) = refs
     else:
         acc_ref, m_ref = refs
     me = {axis: lax.axis_index(axis) for axis in ("zh", "y", "k", "c")}
-    width = 512
-    y = (me["y"] + steps[0] + steps[1] * me["c"]) % 4
-    ones = jnp.ones((width, 128), jnp.bfloat16)
-    row = lax.broadcasted_iota(jnp.int32, (ROWS, 128), 0)
-    lane = lax.broadcasted_iota(jnp.int32, (ROWS, 128), 1)
     pair = me["zh"] * 2 + me["k"]
-    turns = (0, 3 - 2 * me["c"], 2, 1 + 2 * me["c"])
-    turn = functools.reduce(
-        lambda so_far, j: jnp.where(row // 128 == j, turns[j], so_far), range(1, 4), row * 0
-    )
+    every_turn = (0, 3 - 2 * me["c"], 1 + 2 * me["c"], 2)
+    turns = [every_turn[group] for groups in sets for group in groups]
+    size = 128 * len(turns)
+    ones = jnp.ones((512, 128), jnp.bfloat16)
+    row = lax.broadcasted_iota(jnp.int32, (size, 128), 0)
+    lane = lax.broadcasted_iota(jnp.int32, (size, 128), 1)
+    turn = row * 0 + turns[0]
+    for j in range(1, len(turns)):
+        turn = jnp.where(row // 128 == j, turns[j], turn)
     z = (pair + turn) % 4
     q_dev = (z // 2) * 32 + me["y"] * 8 + (z % 2) * 4 + (row // 64 % 2) * 2 + me["c"]
     reach = q_dev * 128 + 120 + (row % 64) // 8 - lane
-    queries, state = {}, {}
-    for xq in range(4):
-        rows = slice(xq * ROWS, (xq + 1) * ROWS)
-        queries[xq] = q_ref[rows]
-        state[xq] = None if first else (m_in[rows], acc_in[rows])
-
-    def gathered(xk, kind):
+
+    def joined(some_refs, xq):
         found = []
-        for kv_ref in kv_refs:
+        for groups, ref in zip(sets, some_refs):
+            rows = 128 * len(groups)
+            found.append(ref[xq * rows : (xq + 1) * rows])
+        return found[0] if len(found) == 1 else jnp.concatenate(found, axis=0)
+
+    queries = [joined(q_refs, xq) for xq in range(4)]
+    state = [None] * 4
+    if not first:
+        for xq in range(4):
+            acc = joined([acc_in for acc_in, _ in states_in], xq)
+            state[xq] = (joined([m_in for _, m_in in states_in], xq), acc)
+
+    def gathered(source, xk, kind):
+        found = []
+        for kv_ref in kv_refs[source]:
             rows = kv_ref[xk * 2 : xk * 2 + 2, kind * 128 : (kind + 1) * 128]
             found.append(rows.reshape(256, 128))
         return jnp.concatenate(found, axis=0)
 
-    def score(xq, xk):
-        keys = gathered(xk, 0)
+    def score(source, xqs, xk):
+        keys = gathered(source, xk, 0)
         return lax.dot_general(
-            queries[xq],
+            jnp.concatenate([queries[xq] for xq in xqs], axis=0),
             jnp.concatenate([keys, keys], axis=1),
             (((1,), (1,)), ((), ())),
             preferred_element_type=jnp.float32,
         )
 
-    def absorb(xq, xk, scores):
-        parts = [scores[:, j * 128 : (j + 1) * 128] for j in range(width // 128)]
-        if xk == xq:
-            for j in range(width // 128):
-                core = me["c"] if j // 2 == swapped else 1 - me["c"]
-                k_dev = me["zh"] * 32 + y * 8 + me["k"] * 4 + j % 2 * 2 + core
-                parts[j] = jnp.where(reach >= k_dev * 128, parts[j], NEVER)
-        top = jnp.max(functools.reduce(jnp.maximum, parts), axis=1, keepdims=True)
-        if state[xq] is None:
-            new = jnp.broadcast_to(top, (ROWS, 128))
-        else:
-            new = jnp.maximum(state[xq][0], top)
-        weights = jnp.concatenate(
-            [jnp.exp2(part - new).astype(jnp.bfloat16) for part in parts], axis=1
+    def absorb(source, xqs, xk, scores):
+        steps, swapped, _ = sources[source]
+        y = (me["y"] + steps[0] + steps[1] * me["c"]) % 4
+        weights, maxima = [], []
+        for i, xq in enumerate(xqs):
+            mine = scores[i * size : (i + 1) * size]
+            parts = [mine[:, j * 128 : (j + 1) * 128] for j in range(4)]
+            if xk == xq:
+                for j in range(4):
+                    core = me["c"] if j // 2 == swapped else 1 - me["c"]
+                    k_dev = me["zh"] * 32 + y * 8 + me["k"] * 4 + j % 2 * 2 + core
+                    parts[j] = jnp.where(reach >= k_dev * 128, parts[j], NEVER)
+            top = jnp.max(functools.reduce(jnp.maximum, parts), axis=1, keepdims=True)
+            if state[xq] is None:
+                new = jnp.broadcast_to(top, (size, 128))
+            else:
+                new = jnp.maximum(state[xq][0], top)
+            maxima.append(new)
+            exponents = [jnp.exp2(part - new).astype(jnp.bfloat16) for part in parts]
+            weights.append(jnp.concatenate(exponents, axis=1))
+        values = gathered(source, xk, 1)
+        added = jnp.dot(
+            jnp.concatenate(weights, axis=0),
+            jnp.concatenate([values, ones], axis=1),
+            preferred_element_type=jnp.float32,
         )
-        values = gathered(xk, 1)
-        acc = jnp.dot(
-            weights, jnp.concatenate([values, ones], axis=1), preferred_element_type=jnp.float32
-        )
-        if state[xq] is not None:
-            shrink = jnp.exp2(state[xq][0] - new)
-            acc = state[xq][1] * jnp.concatenate([shrink, shrink], axis=1) + acc
-        state[xq] = (new, acc)
+        for i, (xq, new) in enumerate(zip(xqs, maxima)):
+            acc = added[i * size : (i + 1) * size]
+            if state[xq] is not None:
+                shrink = jnp.exp2(state[xq][0] - new)
+                acc = state[xq][1] * jnp.concatenate([shrink, shrink], axis=1) + acc
+            state[xq] = (new, acc)
 
     def finish(xq):
         maxima, acc = state[xq]
         if not last:
-            m_ref[xq * ROWS : (xq + 1) * ROWS] = maxima
-            acc_ref[xq * ROWS : (xq + 1) * ROWS] = acc
+            m_ref[xq * size : (xq + 1) * size] = maxima
+            acc_ref[xq * size : (xq + 1) * size] = acc
             return
         totals = acc[:, 128:]
         result = (acc[:, :128] / totals).astype(jnp.bfloat16)
@@ -185,13 +210,16 @@
             stats = jnp.where(stat_row == 0, one, jnp.where(stat_row == 1, two, stats))
             send_ref[chunk, 64:80] = stats.astype(jnp.bfloat16)
 
-    order = [(3, 0), (2, 0), (1, 0), (0, 0), (3, 1), (2, 1), (1, 1), (3, 2), (2, 2), (3, 3)]
-    scores = score(*order[0])
-    for now, later in zip(order, order[1:] + [None]):
-        ahead = None if later is None else score(*later)
-        absorb(*now, scores)
-        if now[0] == now[1]:
-            finish(now[0])
+    order = ONE_BY_ONE if size > 128 else STACKED
+    work = [(source, *tile) for source in range(len(sources)) for tile in order]
+    scores = score(*work[0])
+    for i, (source, xqs, xk) in enumerate(work):
+        ahead = score(*work[i + 1]) if i + 1 < len(work) else None
+        absorb(source, xqs, xk, scores)
+        if source == len(sources) - 1:
+            for xq in xqs:
+                if xq == xk:
+                    finish(xq)
         scores = ahead
 
 
@@ -276,33 +304,33 @@
     q_across = apart(q_near, ("zh", "k"))
     kv_own = jnp.concatenate([kv, swap(kv)], axis=0)
     kv_near = apart(kv_own, ("y",))
-    kv_far = swap(kv_near)
-    kv_across = apart(kv_near[:8], ("y",))
-    q_all = pl.pallas_call(
-        scale_kernel,
-        out_shape=jax.ShapeDtypeStruct((2048, 256), jnp.bfloat16),
-        in_specs=[VMEM] * 4,
-        out_specs=VMEM,
-        compiler_params=params(),
-        cost_estimate=cost(2**20, 0, 2**21),
-        name="scale_queries",
-    )(q_mine, q_near, q_across, q_far)
-
-    def attend(name, steps, swapped, values, state, weight=4):
+    def scaled(*values):
+        return pl.pallas_call(
+            scale_kernel,
+            out_shape=jax.ShapeDtypeStruct((512 * len(values), 256), jnp.bfloat16),
+            in_specs=[VMEM] * len(values),
+            out_specs=VMEM,
+            compiler_params=params(),
+            cost_estimate=cost(2**20, 0, 2**21),
+            name="scale_queries",
+        )(*values)
+
+    q_first = scaled(q_mine, q_near, q_far)
+
+    def attend(name, sets, q_sets, sources, values, states, weight=4):
         last = name == "attend_d"
         if last:
             out_shape, out_specs = jax.ShapeDtypeStruct((32, 80, 128), jnp.bfloat16), VMEM
         else:
+            rows = 512 * len(sets[0])
             out_shape = (
-                jax.ShapeDtypeStruct((2048, 256), jnp.float32),
-                jax.ShapeDtypeStruct((2048, 128), jnp.float32),
+                jax.ShapeDtypeStruct((rows, 256), jnp.float32),
+                jax.ShapeDtypeStruct((rows, 128), jnp.float32),
             )
             out_specs = (VMEM, VMEM)
-        operands = (q_all, *values, *state)
+        operands = (*q_sets, *values, *(part for state in states for part in state))
         return pl.pallas_call(
-            functools.partial(
-                attend_kernel, steps, swapped, len(values) == 1, not state, last
-            ),
+            functools.partial(attend_kernel, sets, sources, not states, last),
             out_shape=out_shape,
             in_specs=[VMEM] * len(operands),
             out_specs=out_specs,
@@ -311,10 +339,28 @@
             name=name,
         )(*operands)
 
-    state = attend("attend_a", (0, 0), 0, (kv_own,), ())
-    state = attend("attend_b", (3, -2), 0, (kv_near,), state)
-    state = attend("attend_c", (1, 2), 1, (kv_far,), state, 16)
-    o_send = attend("attend_d", (2, 0), 0, (kv_across, swap(kv_across)), state)
+    own, near, far = ((0, 0), 0, True), ((3, -2), 0, True), ((1, 2), 1, True)
+    across = ((2, 0), 0, False)
+    one, two = (FIRST_SET,), (SECOND_SET,)
+    state = attend("attend_a", one, [q_first], (own,), (kv_own,), [])
+    kv_near, state = lax.optimization_barrier((kv_near, state))
+    kv_far = swap(kv_near)
+    kv_across = apart(kv_near[:8], ("y",))
+    state = attend("attend_b", one, [q_first], (near,), (kv_near,), [state])
+    state = attend("attend_c", one, [q_first], (far,), (kv_far,), [state], 2)
+    q_across, kv_across, state = lax.optimization_barrier((q_across, kv_across, state))
+    q_second = scaled(q_across)
+    extra = attend(
+        "attend_e", two, [q_second], (own, near, far), (kv_own, kv_near, kv_far), [], 16
+    )
+    o_send = attend(
+        "attend_d",
+        (FIRST_SET, SECOND_SET),
+        [q_first, q_second],
+        (across,),
+        (kv_across, swap(kv_across)),
+        [state, extra],
+    )
     o_recv = lax.all_to_all(o_send, QUERY_GROUP, 0, 0, tiled=True)
     return pl.pallas_call(
         combine_kernel,

time: 96.8 us -> 92.6 us (0.957)
  waiting for transfers between devices: 18.8 us -> 16 us
  starting transfers between devices: 8.6 us -> 6.38 us
    ppermute x4, waiting for transfers between devices: 15.7 us -> 13.4 us  [apart(): return lax.ppermute(value, (*axis, 'c'), turns)]
    ppermute x5, starting transfers between devices: 3.26 us -> 1.08 us  [swap(): return lax.ppermute(value, 'c', [(0, 1), (1, 0)])]
    pallas_call x5 -> x7, Pallas kernels: 14.5 us -> 14.8 us  [the longest x5 14.6 us: attend(): pl.pallas_call(functools.partial(attend_kernel, sets, sources, not states...]
  transfers between devices with their start and end apart: 10 -> 10, of which waited for: 4 -> 6; matrix products, arithmetic and copies ran while one was open for 0% -> 0% of each run, Pallas kernels for 12% -> 13%
where the time goes in v3:
time: 92.6 us; the launch traced here: 92.4 us
  blocking collectives  48.3 us (52%)
  Pallas kernels  17.8 us (19%)
  waiting for transfers between devices  16 us (17%)
  starting transfers between devices  6.38 us (7%)
  local copies, waits for them, and re-layouts  3.64 us (4%)
    all_to_all x1, blocking collectives, on_device(): o_recv = lax.all_to_all(o_send, QUERY_GROUP, 0, 0, tiled=True)  28.1 us
    all_to_all x1, blocking collectives, on_device(): received = lax.all_to_all(send, ('x', 'zp'), 0, 0, tiled=True)  20.2 us
    pallas_call x5, Pallas kernels, attend(): pl.pallas_call(functools.partial(attend_kernel, sets, sources, not states...  14.6 us
    ppermute x4, waiting for transfers between devices, apart(): return lax.ppermute(value, (*axis, 'c'), turns)  13.4 us
    unnamed x8, local copies, waits for them, and re-layouts  3.54 us
    ppermute x4, starting transfers between devices, apart(): return lax.ppermute(value, (*axis, 'c'), turns)  3.39 us
    ppermute x5, waiting for transfers between devices, swap(): return lax.ppermute(value, 'c', [(0, 1), (1, 0)])  2.64 us
    ppermute x1, starting transfers between devices, on_device(): lax.ppermute(visual_keyval, AXES, [(i, i - 1) for i in range(1, owners)])  1.91 us
  transfers between devices with their start and end apart: 10, of which 6 were waited for; matrix products, arithmetic and copies ran while one was open for 0% of the time, Pallas kernels for 13%

profile of v3, /device:TPU:32, one launch (start us, length us, event | category | flops | bytes accessed | tf_op | source)
XLA Modules:
  0.0 92.4 jit_solution(13981014171423313027)
XLA Ops:
  0.0 1.9 %collective-permute-start = (bf16[48,8,2,128]{3,2,1,0:T(2,128)(2,1)}, bf16[48,8,2,128]{3,2,1,0:T(2,128)(2,1)S(1)}, u32[]{:S(2)}, u32[]{:S(2)}) collective-permute-start(bf16[48,8,2,128]{3,2,1,0:T(2,128)(2,1)} %param.6), channel_id=1, source_target_pairs={{1,0},{2,1},{3,2},{4,3},{5,4},{6,5},{7,6},{8,7},{9,8},{10,9},{11,1... | collective-permute-start | bytes 589832 | tf_op jit(solution)/shard_map/ppermute | solution.py:260
  1.9 1.0 %copy-done = bf16[128,8,2,128]{3,2,1,0:T(2,128)(2,1)S(1)} copy-done((bf16[128,8,2,128]{3,2,1,0:T(2,128)(2,1)S(1)}, bf16[128,8,2,128]{3,2,1,0:T(2,128)(2,1)}, u32[]{:S(2)}) %copy-start) | copy-done | bytes 524312
  3.0 0.9 %copy-done.1 = bf16[48,8,2,128]{3,2,1,0:T(2,128)(2,1)S(1)} copy-done((bf16[48,8,2,128]{3,2,1,0:T(2,128)(2,1)S(1)}, bf16[48,8,2,128]{3,2,1,0:T(2,128)(2,1)}, u32[]{:S(2)}) %copy-start.1) | copy-done | bytes 196632
  3.9 0.9 copy-done.2
  4.8 0.7 copy-done.3
  5.5 1.0 %local_rows.1 = (bf16[8,64,128]{2,1,0:T(8,128)(2,1)S(1)}, bf16[2048,128]{1,0:T(8,128)(2,1)S(1)}, bf16[768,128]{1,0:T(8,128)(2,1)S(1)}, s32[2]{0:T(128)S(1)}) custom-call(s32[2,128]{1,0:T(2,128)S(1)} %bitcast.11, bf16[8,64,128]{2,1,0:T(8,128)(2,1)S(1)} %copy-done.2, bf16[2048,128]{1,0:T(8,128)(2,1)S(1)} %bitcast.8, bf16[768,128]{1,0:T(8,128)(2,1)S(1)} %bitcast.10), custom_call_target="tpu_custom_call" | custom-call | flops 134217728 | bytes 3145728 | tf_op jit(solution)/shard_map/local_rows/pallas_call | solution.py:261
  6.5 1.0 %place_rows.1 = bf16[8,320,128]{2,1,0:T(8,128)(2,1)S(1)} custom-call(s32[2]{0:T(128)S(1)} %get-tuple-element.24.window_ref, bf16[8,64,128]{2,1,0:T(8,128)(2,1)S(1)} %get-tuple-element.25.q_ref, bf16[2048,128]{1,0:T(8,128)(2,1)S(1)} %get-tuple-element.26.moved_ref, bf16[768,128]{1,0:T(8,128)(2,1)S(1)} %get-tuple-element.27.vis_ref, bf16[768,128]{1,0:T(8,128)(2,1)S(1)} %bitcast.9), custom_call_target="tpu_custom_call" | custom-call | flops 100663296 | bytes 2097152 | tf_op jit(solution)/shard_map/place_rows/pallas_call | solution.py:280
  7.5 20.2 %all_to_all.10 = bf16[8,320,128]{2,1,0:T(8,128)(2,1)S(1)} all-to-all(bf16[8,320,128]{2,1,0:T(8,128)(2,1)S(1)} %place_rows.1), channel_id=1, replica_groups=mesh['x'=4,'zh'=2,'y'=4,'k'=2,'zp'=2,'c'=2] {'x','zp'}, dimensions={0} | all-to-all | bytes 1310720 | tf_op jit(solution)/shard_map/all_to_all | solution.py:290
  27.7 0.1 collective-permute-start.5
  27.8 0.6 collective-permute-start.1
  28.3 1.3 %collective-permute-done.5 = bf16[8,256,128]{2,1,0:T(8,128)(2,1)S(1)} collective-permute-done((bf16[8,256,128]{2,1,0:T(8,128)(2,1)S(1)}, bf16[8,256,128]{2,1,0:T(8,128)(2,1)S(1)}, u32[]{:S(2)}, u32[]{:S(2)}) %collective-permute-start.5) | collective-permute-done | bytes 524320 | tf_op jit(solution)/shard_map/ppermute | solution.py:299
  29.6 0.1 pad_maximum_fusion.refs_1_
  29.7 0.1 collective-permute-start.6
  29.9 1.5 %collective-permute-start.2 = (bf16[1024,128]{1,0:T(8,128)(2,1)S(1)}, bf16[1024,128]{1,0:T(8,128)(2,1)S(1)}, u32[]{:S(2)}, u32[]{:S(2)}) collective-permute-start(bf16[1024,128]{1,0:T(8,128)(2,1)S(1)} %pad_maximum_fusion.1), channel_id=1, source_target_pairs={{0,4},{1,37},{4,32},{5,1},{32,36},{33,5},{36,0},{37,33},{2,6},{3,3... | collective-permute-start | bytes 786440 | tf_op jit(solution)/shard_map/ppermute | solution.py:296
  31.3 9.9 %collective-permute-done.2 = bf16[1024,128]{1,0:T(8,128)(2,1)S(1)} collective-permute-done((bf16[1024,128]{1,0:T(8,128)(2,1)S(1)}, bf16[1024,128]{1,0:T(8,128)(2,1)S(1)}, u32[]{:S(2)}, u32[]{:S(2)}) %collective-permute-start.2) | collective-permute-done | bytes 262176 | tf_op jit(solution)/shard_map/ppermute | solution.py:296
  41.3 0.1 collective-permute-start.3
  41.4 1.3 %collective-permute-done.3.refs_2_ = bf16[512,128]{1,0:T(8,128)(2,1)S(1)} collective-permute-done((bf16[512,128]{1,0:T(8,128)(2,1)S(1)}, bf16[512,128]{1,0:T(8,128)(2,1)S(1)}, u32[]{:S(2)}, u32[]{:S(2)}) %collective-permute-start.3) | collective-permute-done | bytes 131104 | tf_op jit(solution)/shard_map/ppermute | solution.py:299
  42.7 0.1 scale_queries.2.refs_0_
  42.8 2.6 %attend_a.1 = (f32[1536,256]{1,0:T(8,128)S(1)}, f32[1536,128]{1,0:T(8,128)S(1)}) custom-call(bf16[1536,256]{1,0:T(8,128)(2,1)S(1)} %scale_queries.2.refs_0_, bf16[16,256,128]{2,1,0:T(8,128)(2,1)S(1)} %pad_maximum_fusion.refs_1_), custom_call_target="tpu_custom_call" | custom-call | flops 2684354560 | bytes 6291456 | tf_op jit(solution)/shard_map/attend_a/pallas_call | solution.py:332
  45.5 0.4 collective-permute-done.6.refs_1_.refs_2_
  45.9 1.4 %collective-permute-start.7 = (bf16[8,256,128]{2,1,0:T(8,128)(2,1)S(1)}, bf16[8,256,128]{2,1,0:T(8,128)(2,1)S(1)}, u32[]{:S(2)}, u32[]{:S(2)}) collective-permute-start(bf16[8,256,128]{2,1,0:T(8,128)(2,1)S(1)} %slice.19), channel_id=1, source_target_pairs={{0,8},{1,25},{8,16},{9,1},{16,24},{17,9},{24,0},{25,17},{2,10},{3,... | collective-permute-start | bytes 1572872 | tf_op jit(solution)/shard_map/ppermute | solution.py:296
  47.3 0.5 collective-permute-start.4
  47.7 2.8 %attend_b.1 = (f32[1536,256]{1,0:T(8,128)S(1)}, f32[1536,128]{1,0:T(8,128)S(1)}) custom-call(bf16[1536,256]{1,0:T(8,128)(2,1)S(1)} %scale_queries.2.refs_0_, bf16[16,256,128]{2,1,0:T(8,128)(2,1)S(1)} %collective-permute-done.6.refs_1_.refs_2_, f32[1536,256]{1,0:T(8,128)S(1)} %get-tuple-element.31.refs_2_, f32[1536,128]{1,0:T(8,128)S(1)} %get-tuple-element.32.refs_3_), custom_call_target="tpu_custom_call" | custom-call | flops 2684354560 | bytes 6291456 | tf_op jit(solution)/shard_map/attend_b/pallas_call | solution.py:332
  50.5 2.8 %attend_c.1 = (f32[1536,256]{1,0:T(8,128)S(1)}, f32[1536,128]{1,0:T(8,128)S(1)}) custom-call(bf16[1536,256]{1,0:T(8,128)(2,1)S(1)} %scale_queries.2.refs_0_, bf16[16,256,128]{2,1,0:T(8,128)(2,1)S(1)} %collective-permute-done.8.refs_1_.refs_3_, f32[1536,256]{1,0:T(8,128)S(1)} %get-tuple-element.33.refs_2_, f32[1536,128]{1,0:T(8,128)S(1)} %get-tuple-element.34.refs_3_), custom_call_target="tpu_custom_call" | custom-call | flops 1342177280 | bytes 6291456 | tf_op jit(solution)/shard_map/attend_c/pallas_call | solution.py:332
  53.2 2.2 %collective-permute-done.4.refs_0_ = bf16[512,128]{1,0:T(8,128)(2,1)S(1)} collective-permute-done((bf16[512,128]{1,0:T(8,128)(2,1)S(1)}, bf16[512,128]{1,0:T(8,128)(2,1)S(1)}, u32[]{:S(2)}, u32[]{:S(2)}) %collective-permute-start.4) | collective-permute-done | bytes 131104 | tf_op jit(solution)/shard_map/ppermute | solution.py:296
  55.4 0.9 collective-permute-done.7.refs_2_
  56.3 0.1 scale_queries.3.refs_0_.refs_1_
  56.4 0.3 collective-permute-start.9
  56.7 2.7 %attend_e.1 = (f32[512,256]{1,0:T(8,128)S(1)}, f32[512,128]{1,0:T(8,128)S(1)}) custom-call(bf16[512,256]{1,0:T(8,128)(2,1)S(1)} %scale_queries.3.refs_0_.refs_1_, bf16[16,256,128]{2,1,0:T(8,128)(2,1)S(1)} %pad_maximum_fusion.refs_1_, bf16[16,256,128]{2,1,0:T(8,128)(2,1)S(1)} %collective-permute-done.6.refs_1_.refs_2_, ...), custom_call_target="tpu_custom_call" | custom-call | flops 10737418240 | bytes 6291456 | tf_op jit(solution)/shard_map/attend_e/pallas_call | solution.py:332
  59.5 3.7 %attend_d.1 = bf16[32,80,128]{2,1,0:T(8,128)(2,1)S(1)} custom-call(bf16[1536,256]{1,0:T(8,128)(2,1)S(1)} %scale_queries.2.refs_0_, bf16[512,256]{1,0:T(8,128)(2,1)S(1)} %scale_queries.3.refs_0_.refs_1_, bf16[8,256,128]{2,1,0:T(8,128)(2,1)S(1)} %collective-permute-done.7.refs_2_, bf16[8,256,128]{2,1,0:T(8,128)(2,1)S(1)} %collective-permute-done.9.refs_3_, ...), custom_call_target="tpu_custom_call" | custom-call | flops 2684354560 | bytes 6291456 | tf_op jit(solution)/shard_map/attend_d/pallas_call | solution.py:332
  63.2 28.1 %all_to_all.11.recv_ref = bf16[32,80,128]{2,1,0:T(8,128)(2,1)S(1)} all-to-all(bf16[32,80,128]{2,1,0:T(8,128)(2,1)S(1)} %attend_d.1), channel_id=1, replica_groups=mesh['x'=4,'zh'=2,'y'=4,'k'=2,'zp'=2,'c'=2] {'x','zh','k','zp'}, dimensions={0} | all-to-all | bytes 1310720 | tf_op jit(solution)/shard_map/all_to_all | solution.py:364
  91.3 1.0 %combine_parts.1 = bf16[8,64,128]{2,1,0:T(8,128)(2,1)} custom-call(bf16[32,80,128]{2,1,0:T(8,128)(2,1)S(1)} %all_to_all.11.recv_ref), custom_call_target="tpu_custom_call" | custom-call | flops 1048576 | bytes 1048576 | tf_op jit(solution)/shard_map/combine_parts/pallas_call | solution.py:365
  (14 shorter events, 0.1 us)
Async XLA Ops:
  0.0 6.5 %collective-permute-start = (bf16[48,8,2,128]{3,2,1,0:T(2,128)(2,1)}, bf16[48,8,2,128]{3,2,1,0:T(2,128)(2,1)S(1)}, u32[]{:S(2)}, u32[]{:S(2)}) collective-permute-start(bf16[48,8,2,128]{3,2,1,0:T(2,128)(2,1)} %param.6), channel_id=1, source_target_pairs={{1,0},{2,1},{3,2},{4,3},{5,4},{6,5},{7,6},{8,7},{9,8},{10,9},{11,1... | collective-permute-start | bytes 589832 | tf_op jit(solution)/shard_map/ppermute | solution.py:260
  1.9 1.0 %copy-start = (bf16[128,8,2,128]{3,2,1,0:T(2,128)(2,1)S(1)}, bf16[128,8,2,128]{3,2,1,0:T(2,128)(2,1)}, u32[]{:S(2)}) copy-start(bf16[128,8,2,128]{3,2,1,0:T(2,128)(2,1)} %param.5) | copy-start | bytes 1572868
  3.0 0.9 %copy-start.1 = (bf16[48,8,2,128]{3,2,1,0:T(2,128)(2,1)S(1)}, bf16[48,8,2,128]{3,2,1,0:T(2,128)(2,1)}, u32[]{:S(2)}) copy-start(bf16[48,8,2,128]{3,2,1,0:T(2,128)(2,1)} %param.6) | copy-start | bytes 589828
  3.9 0.9 copy-start.2
  4.8 0.7 copy-start.3
  27.7 2.0 %collective-permute-start.5 = (bf16[8,256,128]{2,1,0:T(8,128)(2,1)S(1)}, bf16[8,256,128]{2,1,0:T(8,128)(2,1)S(1)}, u32[]{:S(2)}, u32[]{:S(2)}) collective-permute-start(bf16[8,256,128]{2,1,0:T(8,128)(2,1)S(1)} %slice.23), channel_id=1, source_target_pairs={{0,1},{1,0},{2,3},{3,2},{4,5},{5,4},{6,7},{7,6},{8,9},{9,8},{10,11... | collective-permute-start | bytes 1572872 | tf_op jit(solution)/shard_map/ppermute | solution.py:299
  27.8 2.1 %collective-permute-start.1 = (bf16[512,128]{1,0:T(8,128)(2,1)S(1)}, bf16[512,128]{1,0:T(8,128)(2,1)S(1)}, u32[]{:S(2)}, u32[]{:S(2)}) collective-permute-start(bf16[512,128]{1,0:T(8,128)(2,1)S(1)} %bitcast.5), channel_id=1, source_target_pairs={{0,1},{1,0},{2,3},{3,2},{4,5},{5,4},{6,7},{7,6},{8,9},{9,8},{10,11... | collective-permute-start | bytes 393224 | tf_op jit(solution)/shard_map/ppermute | solution.py:299
  29.7 16.1 %collective-permute-start.6 = (bf16[16,256,128]{2,1,0:T(8,128)(2,1)S(1)}, bf16[16,256,128]{2,1,0:T(8,128)(2,1)S(1)}, u32[]{:S(2)}, u32[]{:S(2)}) collective-permute-start(bf16[16,256,128]{2,1,0:T(8,128)(2,1)S(1)} %pad_maximum_fusion.refs_1_), channel_id=1, source_target_pairs={{0,8},{1,25},{8,16},{9,1},{16,24},{17,9},{24,0},{25,17},{2,10},{3,... | collective-permute-start | bytes 3145736 | tf_op jit(solution)/shard_map/ppermute | solution.py:296
  29.9 11.4 %collective-permute-start.2 = (bf16[1024,128]{1,0:T(8,128)(2,1)S(1)}, bf16[1024,128]{1,0:T(8,128)(2,1)S(1)}, u32[]{:S(2)}, u32[]{:S(2)}) collective-permute-start(bf16[1024,128]{1,0:T(8,128)(2,1)S(1)} %pad_maximum_fusion.1), channel_id=1, source_target_pairs={{0,4},{1,37},{4,32},{5,1},{32,36},{33,5},{36,0},{37,33},{2,6},{3,3... | collective-permute-start | bytes 786440 | tf_op jit(solution)/shard_map/ppermute | solution.py:296
  41.3 1.4 %collective-permute-start.3 = (bf16[512,128]{1,0:T(8,128)(2,1)S(1)}, bf16[512,128]{1,0:T(8,128)(2,1)S(1)}, u32[]{:S(2)}, u32[]{:S(2)}) collective-permute-start(bf16[512,128]{1,0:T(8,128)(2,1)S(1)} %get-tuple-element.43), channel_id=1, source_target_pairs={{0,1},{1,0},{2,3},{3,2},{4,5},{5,4},{6,7},{7,6},{8,9},{9,8},{10,11... | collective-permute-start | bytes 393224 | tf_op jit(solution)/shard_map/ppermute | solution.py:299
  45.8 4.6 %collective-permute-start.8 = (bf16[16,256,128]{2,1,0:T(8,128)(2,1)S(1)}, bf16[16,256,128]{2,1,0:T(8,128)(2,1)S(1)}, u32[]{:S(2)}, u32[]{:S(2)}) collective-permute-start(bf16[16,256,128]{2,1,0:T(8,128)(2,1)S(1)} %collective-permute-done.6.refs_1_.refs_2_), channel_id=1, source_target_pairs={{0,1},{1,0},{2,3},{3,2},{4,5},{5,4},{6,7},{7,6},{8,9},{9,8},{10,11... | collective-permute-start | bytes 3145736 | tf_op jit(solution)/shard_map/ppermute | solution.py:299
  45.9 10.5 %collective-permute-start.7 = (bf16[8,256,128]{2,1,0:T(8,128)(2,1)S(1)}, bf16[8,256,128]{2,1,0:T(8,128)(2,1)S(1)}, u32[]{:S(2)}, u32[]{:S(2)}) collective-permute-start(bf16[8,256,128]{2,1,0:T(8,128)(2,1)S(1)} %slice.19), channel_id=1, source_target_pairs={{0,8},{1,25},{8,16},{9,1},{16,24},{17,9},{24,0},{25,17},{2,10},{3,... | collective-permute-start | bytes 1572872 | tf_op jit(solution)/shard_map/ppermute | solution.py:296
  47.3 8.2 %collective-permute-start.4 = (bf16[512,128]{1,0:T(8,128)(2,1)S(1)}, bf16[512,128]{1,0:T(8,128)(2,1)S(1)}, u32[]{:S(2)}, u32[]{:S(2)}) collective-permute-start(bf16[512,128]{1,0:T(8,128)(2,1)S(1)} %get-tuple-element.44.refs_1_), channel_id=1, source_target_pairs={{0,4},{1,37},{4,32},{5,1},{32,36},{33,5},{36,0},{37,33},{2,6},{3,3... | collective-permute-start | bytes 393224 | tf_op jit(solution)/shard_map/ppermute | solution.py:296
  56.4 3.1 %collective-permute-start.9 = (bf16[8,256,128]{2,1,0:T(8,128)(2,1)S(1)}, bf16[8,256,128]{2,1,0:T(8,128)(2,1)S(1)}, u32[]{:S(2)}, u32[]{:S(2)}) collective-permute-start(bf16[8,256,128]{2,1,0:T(8,128)(2,1)S(1)} %collective-permute-done.7.refs_2_), channel_id=1, source_target_pairs={{0,1},{1,0},{2,3},{3,2},{4,5},{5,4},{6,7},{7,6},{8,9},{9,8},{10,11... | collective-permute-start | bytes 1572872 | tf_op jit(solution)/shard_map/ppermute | solution.py:299

commit v4 on v3

--- a/solution.py
+++ b/solution.py
@@ -224,9 +224,9 @@
 
 
 def combine_kernel(recv_ref, out_ref):
-    eye = lax.broadcasted_iota(jnp.int32, (64, 128), 0) == lax.broadcasted_iota(
-        jnp.int32, (64, 128), 1
-    )
+    row = lax.broadcasted_iota(jnp.int32, (64, 256), 0)
+    lane = lax.broadcasted_iota(jnp.int32, (64, 256), 1)
+    diagonal = lane % 64 == row
     for x in range(4):
         heads = []
         for zp in range(2):
@@ -238,11 +238,16 @@
             top = functools.reduce(jnp.maximum, levels)
             shares = [jnp.exp2(level - top) for level in levels]
             whole = functools.reduce(jnp.add, shares)
-            total = None
-            for chunk, share in zip(chunks, shares):
-                column = jnp.sum(jnp.where(eye, share / whole, 0.0), axis=1, keepdims=True)
-                term = recv_ref[chunk, :64].astype(jnp.float32) * column
-                total = term if total is None else total + term
+            line = jnp.concatenate([(share / whole)[:, :64] for share in shares], axis=1)
+            weights = jnp.where(diagonal, line, 0.0)
+            high = weights.astype(jnp.bfloat16)
+            low = (weights - high.astype(jnp.float32)).astype(jnp.bfloat16)
+            data = jnp.concatenate([recv_ref[chunk, :64] for chunk in chunks], axis=0)
+            total = jnp.dot(
+                jnp.concatenate([high, low], axis=1),
+                jnp.concatenate([data, data], axis=0),
+                preferred_element_type=jnp.float32,
+            )
             heads.append(total.reshape(8, 8, 128))
         out_ref[:, x * 16 : (x + 1) * 16, :] = jnp.concatenate(heads, axis=1).astype(jnp.bfloat16)
 

time: 92.6 us -> 92.6 us (level)
  no operation moved by 1% of the time
where the time goes in v4:
time: 92.6 us; the launch traced here: 92.4 us
  blocking collectives  48.3 us (52%)
  Pallas kernels  17.8 us (19%)
  waiting for transfers between devices  16 us (17%)
  starting transfers between devices  6.38 us (7%)
  local copies, waits for them, and re-layouts  3.64 us (4%)
    all_to_all x1, blocking collectives, on_device(): o_recv = lax.all_to_all(o_send, QUERY_GROUP, 0, 0, tiled=True)  28.1 us
    all_to_all x1, blocking collectives, on_device(): received = lax.all_to_all(send, ('x', 'zp'), 0, 0, tiled=True)  20.2 us
    pallas_call x5, Pallas kernels, attend(): pl.pallas_call(functools.partial(attend_kernel, sets, sources, not states...  14.6 us
    ppermute x4, waiting for transfers between devices, apart(): return lax.ppermute(value, (*axis, 'c'), turns)  13.4 us
    unnamed x8, local copies, waits for them, and re-layouts  3.54 us
    ppermute x4, starting transfers between devices, apart(): return lax.ppermute(value, (*axis, 'c'), turns)  3.39 us
    ppermute x5, waiting for transfers between devices, swap(): return lax.ppermute(value, 'c', [(0, 1), (1, 0)])  2.64 us
    ppermute x1, starting transfers between devices, on_device(): lax.ppermute(visual_keyval, AXES, [(i, i - 1) for i in range(1, owners)])  1.91 us
  transfers between devices with their start and end apart: 10, of which 6 were waited for; matrix products, arithmetic and copies ran while one was open for 0% of the time, Pallas kernels for 13%

profile of v4, /device:TPU:32, one launch (start us, length us, event | category | flops | bytes accessed | tf_op | source)
XLA Modules:
  0.0 92.4 jit_solution(17243901768064692969)
XLA Ops:
  0.0 1.9 %collective-permute-start = (bf16[48,8,2,128]{3,2,1,0:T(2,128)(2,1)}, bf16[48,8,2,128]{3,2,1,0:T(2,128)(2,1)S(1)}, u32[]{:S(2)}, u32[]{:S(2)}) collective-permute-start(bf16[48,8,2,128]{3,2,1,0:T(2,128)(2,1)} %param.6), channel_id=1, source_target_pairs={{1,0},{2,1},{3,2},{4,3},{5,4},{6,5},{7,6},{8,7},{9,8},{10,9},{11,1... | collective-permute-start | bytes 589832 | tf_op jit(solution)/shard_map/ppermute | solution.py:265
  1.9 1.0 %copy-done = bf16[128,8,2,128]{3,2,1,0:T(2,128)(2,1)S(1)} copy-done((bf16[128,8,2,128]{3,2,1,0:T(2,128)(2,1)S(1)}, bf16[128,8,2,128]{3,2,1,0:T(2,128)(2,1)}, u32[]{:S(2)}) %copy-start) | copy-done | bytes 524312
  3.0 0.9 %copy-done.1 = bf16[48,8,2,128]{3,2,1,0:T(2,128)(2,1)S(1)} copy-done((bf16[48,8,2,128]{3,2,1,0:T(2,128)(2,1)S(1)}, bf16[48,8,2,128]{3,2,1,0:T(2,128)(2,1)}, u32[]{:S(2)}) %copy-start.1) | copy-done | bytes 196632
  3.9 0.9 copy-done.2
  4.8 0.7 copy-done.3
  5.5 1.0 %local_rows.1 = (bf16[8,64,128]{2,1,0:T(8,128)(2,1)S(1)}, bf16[2048,128]{1,0:T(8,128)(2,1)S(1)}, bf16[768,128]{1,0:T(8,128)(2,1)S(1)}, s32[2]{0:T(128)S(1)}) custom-call(s32[2,128]{1,0:T(2,128)S(1)} %bitcast.11, bf16[8,64,128]{2,1,0:T(8,128)(2,1)S(1)} %copy-done.2, bf16[2048,128]{1,0:T(8,128)(2,1)S(1)} %bitcast.8, bf16[768,128]{1,0:T(8,128)(2,1)S(1)} %bitcast.10), custom_call_target="tpu_custom_call" | custom-call | flops 134217728 | bytes 3145728 | tf_op jit(solution)/shard_map/local_rows/pallas_call | solution.py:266
  6.5 1.0 %place_rows.1 = bf16[8,320,128]{2,1,0:T(8,128)(2,1)S(1)} custom-call(s32[2]{0:T(128)S(1)} %get-tuple-element.24.window_ref, bf16[8,64,128]{2,1,0:T(8,128)(2,1)S(1)} %get-tuple-element.25.q_ref, bf16[2048,128]{1,0:T(8,128)(2,1)S(1)} %get-tuple-element.26.moved_ref, bf16[768,128]{1,0:T(8,128)(2,1)S(1)} %get-tuple-element.27.vis_ref, bf16[768,128]{1,0:T(8,128)(2,1)S(1)} %bitcast.9), custom_call_target="tpu_custom_call" | custom-call | flops 100663296 | bytes 2097152 | tf_op jit(solution)/shard_map/place_rows/pallas_call | solution.py:285
  7.5 20.2 %all_to_all.10 = bf16[8,320,128]{2,1,0:T(8,128)(2,1)S(1)} all-to-all(bf16[8,320,128]{2,1,0:T(8,128)(2,1)S(1)} %place_rows.1), channel_id=1, replica_groups=mesh['x'=4,'zh'=2,'y'=4,'k'=2,'zp'=2,'c'=2] {'x','zp'}, dimensions={0} | all-to-all | bytes 1310720 | tf_op jit(solution)/shard_map/all_to_all | solution.py:295
  27.7 0.1 collective-permute-start.5
  27.8 0.6 collective-permute-start.1
  28.3 1.3 %collective-permute-done.5 = bf16[8,256,128]{2,1,0:T(8,128)(2,1)S(1)} collective-permute-done((bf16[8,256,128]{2,1,0:T(8,128)(2,1)S(1)}, bf16[8,256,128]{2,1,0:T(8,128)(2,1)S(1)}, u32[]{:S(2)}, u32[]{:S(2)}) %collective-permute-start.5) | collective-permute-done | bytes 524320 | tf_op jit(solution)/shard_map/ppermute | solution.py:304
  29.6 0.1 pad_maximum_fusion.refs_1_
  29.7 0.1 collective-permute-start.6
  29.9 1.5 %collective-permute-start.2 = (bf16[1024,128]{1,0:T(8,128)(2,1)S(1)}, bf16[1024,128]{1,0:T(8,128)(2,1)S(1)}, u32[]{:S(2)}, u32[]{:S(2)}) collective-permute-start(bf16[1024,128]{1,0:T(8,128)(2,1)S(1)} %pad_maximum_fusion.1), channel_id=1, source_target_pairs={{0,4},{1,37},{4,32},{5,1},{32,36},{33,5},{36,0},{37,33},{2,6},{3,3... | collective-permute-start | bytes 786440 | tf_op jit(solution)/shard_map/ppermute | solution.py:301
  31.3 9.9 %collective-permute-done.2 = bf16[1024,128]{1,0:T(8,128)(2,1)S(1)} collective-permute-done((bf16[1024,128]{1,0:T(8,128)(2,1)S(1)}, bf16[1024,128]{1,0:T(8,128)(2,1)S(1)}, u32[]{:S(2)}, u32[]{:S(2)}) %collective-permute-start.2) | collective-permute-done | bytes 262176 | tf_op jit(solution)/shard_map/ppermute | solution.py:301
  41.3 0.1 collective-permute-start.3
  41.4 1.3 %collective-permute-done.3.refs_2_ = bf16[512,128]{1,0:T(8,128)(2,1)S(1)} collective-permute-done((bf16[512,128]{1,0:T(8,128)(2,1)S(1)}, bf16[512,128]{1,0:T(8,128)(2,1)S(1)}, u32[]{:S(2)}, u32[]{:S(2)}) %collective-permute-start.3) | collective-permute-done | bytes 131104 | tf_op jit(solution)/shard_map/ppermute | solution.py:304
  42.7 0.1 scale_queries.2.refs_0_
  42.8 2.6 %attend_a.1 = (f32[1536,256]{1,0:T(8,128)S(1)}, f32[1536,128]{1,0:T(8,128)S(1)}) custom-call(bf16[1536,256]{1,0:T(8,128)(2,1)S(1)} %scale_queries.2.refs_0_, bf16[16,256,128]{2,1,0:T(8,128)(2,1)S(1)} %pad_maximum_fusion.refs_1_), custom_call_target="tpu_custom_call" | custom-call | flops 2684354560 | bytes 6291456 | tf_op jit(solution)/shard_map/attend_a/pallas_call | solution.py:337
  45.5 0.4 collective-permute-done.6.refs_1_.refs_2_
  45.9 1.4 %collective-permute-start.7 = (bf16[8,256,128]{2,1,0:T(8,128)(2,1)S(1)}, bf16[8,256,128]{2,1,0:T(8,128)(2,1)S(1)}, u32[]{:S(2)}, u32[]{:S(2)}) collective-permute-start(bf16[8,256,128]{2,1,0:T(8,128)(2,1)S(1)} %slice.19), channel_id=1, source_target_pairs={{0,8},{1,25},{8,16},{9,1},{16,24},{17,9},{24,0},{25,17},{2,10},{3,... | collective-permute-start | bytes 1572872 | tf_op jit(solution)/shard_map/ppermute | solution.py:301
  47.3 0.5 collective-permute-start.4
  47.7 2.8 %attend_b.1 = (f32[1536,256]{1,0:T(8,128)S(1)}, f32[1536,128]{1,0:T(8,128)S(1)}) custom-call(bf16[1536,256]{1,0:T(8,128)(2,1)S(1)} %scale_queries.2.refs_0_, bf16[16,256,128]{2,1,0:T(8,128)(2,1)S(1)} %collective-permute-done.6.refs_1_.refs_2_, f32[1536,256]{1,0:T(8,128)S(1)} %get-tuple-element.31.refs_2_, f32[1536,128]{1,0:T(8,128)S(1)} %get-tuple-element.32.refs_3_), custom_call_target="tpu_custom_call" | custom-call | flops 2684354560 | bytes 6291456 | tf_op jit(solution)/shard_map/attend_b/pallas_call | solution.py:337
  50.5 2.8 %attend_c.1 = (f32[1536,256]{1,0:T(8,128)S(1)}, f32[1536,128]{1,0:T(8,128)S(1)}) custom-call(bf16[1536,256]{1,0:T(8,128)(2,1)S(1)} %scale_queries.2.refs_0_, bf16[16,256,128]{2,1,0:T(8,128)(2,1)S(1)} %collective-permute-done.8.refs_1_.refs_3_, f32[1536,256]{1,0:T(8,128)S(1)} %get-tuple-element.33.refs_2_, f32[1536,128]{1,0:T(8,128)S(1)} %get-tuple-element.34.refs_3_), custom_call_target="tpu_custom_call" | custom-call | flops 1342177280 | bytes 6291456 | tf_op jit(solution)/shard_map/attend_c/pallas_call | solution.py:337
  53.2 2.2 %collective-permute-done.4.refs_0_ = bf16[512,128]{1,0:T(8,128)(2,1)S(1)} collective-permute-done((bf16[512,128]{1,0:T(8,128)(2,1)S(1)}, bf16[512,128]{1,0:T(8,128)(2,1)S(1)}, u32[]{:S(2)}, u32[]{:S(2)}) %collective-permute-start.4) | collective-permute-done | bytes 131104 | tf_op jit(solution)/shard_map/ppermute | solution.py:301
  55.4 0.9 collective-permute-done.7.refs_2_
  56.3 0.1 scale_queries.3.refs_0_.refs_1_
  56.4 0.3 collective-permute-start.9
  56.7 2.7 %attend_e.1 = (f32[512,256]{1,0:T(8,128)S(1)}, f32[512,128]{1,0:T(8,128)S(1)}) custom-call(bf16[512,256]{1,0:T(8,128)(2,1)S(1)} %scale_queries.3.refs_0_.refs_1_, bf16[16,256,128]{2,1,0:T(8,128)(2,1)S(1)} %pad_maximum_fusion.refs_1_, bf16[16,256,128]{2,1,0:T(8,128)(2,1)S(1)} %collective-permute-done.6.refs_1_.refs_2_, ...), custom_call_target="tpu_custom_call" | custom-call | flops 10737418240 | bytes 6291456 | tf_op jit(solution)/shard_map/attend_e/pallas_call | solution.py:337
  59.5 3.7 %attend_d.1 = bf16[32,80,128]{2,1,0:T(8,128)(2,1)S(1)} custom-call(bf16[1536,256]{1,0:T(8,128)(2,1)S(1)} %scale_queries.2.refs_0_, bf16[512,256]{1,0:T(8,128)(2,1)S(1)} %scale_queries.3.refs_0_.refs_1_, bf16[8,256,128]{2,1,0:T(8,128)(2,1)S(1)} %collective-permute-done.7.refs_2_, bf16[8,256,128]{2,1,0:T(8,128)(2,1)S(1)} %collective-permute-done.9.refs_3_, ...), custom_call_target="tpu_custom_call" | custom-call | flops 2684354560 | bytes 6291456 | tf_op jit(solution)/shard_map/attend_d/pallas_call | solution.py:337
  63.2 28.1 %all_to_all.11.recv_ref = bf16[32,80,128]{2,1,0:T(8,128)(2,1)S(1)} all-to-all(bf16[32,80,128]{2,1,0:T(8,128)(2,1)S(1)} %attend_d.1), channel_id=1, replica_groups=mesh['x'=4,'zh'=2,'y'=4,'k'=2,'zp'=2,'c'=2] {'x','zh','k','zp'}, dimensions={0} | all-to-all | bytes 1310720 | tf_op jit(solution)/shard_map/all_to_all | solution.py:369
  91.3 1.0 %combine_parts.1 = bf16[8,64,128]{2,1,0:T(8,128)(2,1)} custom-call(bf16[32,80,128]{2,1,0:T(8,128)(2,1)S(1)} %all_to_all.11.recv_ref), custom_call_target="tpu_custom_call" | custom-call | flops 1048576 | bytes 1048576 | tf_op jit(solution)/shard_map/combine_parts/pallas_call | solution.py:370
  (14 shorter events, 0.1 us)
Async XLA Ops:
  0.0 6.5 %collective-permute-start = (bf16[48,8,2,128]{3,2,1,0:T(2,128)(2,1)}, bf16[48,8,2,128]{3,2,1,0:T(2,128)(2,1)S(1)}, u32[]{:S(2)}, u32[]{:S(2)}) collective-permute-start(bf16[48,8,2,128]{3,2,1,0:T(2,128)(2,1)} %param.6), channel_id=1, source_target_pairs={{1,0},{2,1},{3,2},{4,3},{5,4},{6,5},{7,6},{8,7},{9,8},{10,9},{11,1... | collective-permute-start | bytes 589832 | tf_op jit(solution)/shard_map/ppermute | solution.py:265
  1.9 1.0 %copy-start = (bf16[128,8,2,128]{3,2,1,0:T(2,128)(2,1)S(1)}, bf16[128,8,2,128]{3,2,1,0:T(2,128)(2,1)}, u32[]{:S(2)}) copy-start(bf16[128,8,2,128]{3,2,1,0:T(2,128)(2,1)} %param.5) | copy-start | bytes 1572868
  3.0 0.9 %copy-start.1 = (bf16[48,8,2,128]{3,2,1,0:T(2,128)(2,1)S(1)}, bf16[48,8,2,128]{3,2,1,0:T(2,128)(2,1)}, u32[]{:S(2)}) copy-start(bf16[48,8,2,128]{3,2,1,0:T(2,128)(2,1)} %param.6) | copy-start | bytes 589828
  3.9 0.9 copy-start.2
  4.8 0.7 copy-start.3
  27.7 2.0 %collective-permute-start.5 = (bf16[8,256,128]{2,1,0:T(8,128)(2,1)S(1)}, bf16[8,256,128]{2,1,0:T(8,128)(2,1)S(1)}, u32[]{:S(2)}, u32[]{:S(2)}) collective-permute-start(bf16[8,256,128]{2,1,0:T(8,128)(2,1)S(1)} %slice.23), channel_id=1, source_target_pairs={{0,1},{1,0},{2,3},{3,2},{4,5},{5,4},{6,7},{7,6},{8,9},{9,8},{10,11... | collective-permute-start | bytes 1572872 | tf_op jit(solution)/shard_map/ppermute | solution.py:304
  27.8 2.1 %collective-permute-start.1 = (bf16[512,128]{1,0:T(8,128)(2,1)S(1)}, bf16[512,128]{1,0:T(8,128)(2,1)S(1)}, u32[]{:S(2)}, u32[]{:S(2)}) collective-permute-start(bf16[512,128]{1,0:T(8,128)(2,1)S(1)} %bitcast.5), channel_id=1, source_target_pairs={{0,1},{1,0},{2,3},{3,2},{4,5},{5,4},{6,7},{7,6},{8,9},{9,8},{10,11... | collective-permute-start | bytes 393224 | tf_op jit(solution)/shard_map/ppermute | solution.py:304
  29.7 16.1 %collective-permute-start.6 = (bf16[16,256,128]{2,1,0:T(8,128)(2,1)S(1)}, bf16[16,256,128]{2,1,0:T(8,128)(2,1)S(1)}, u32[]{:S(2)}, u32[]{:S(2)}) collective-permute-start(bf16[16,256,128]{2,1,0:T(8,128)(2,1)S(1)} %pad_maximum_fusion.refs_1_), channel_id=1, source_target_pairs={{0,8},{1,25},{8,16},{9,1},{16,24},{17,9},{24,0},{25,17},{2,10},{3,... | collective-permute-start | bytes 3145736 | tf_op jit(solution)/shard_map/ppermute | solution.py:301
  29.9 11.4 %collective-permute-start.2 = (bf16[1024,128]{1,0:T(8,128)(2,1)S(1)}, bf16[1024,128]{1,0:T(8,128)(2,1)S(1)}, u32[]{:S(2)}, u32[]{:S(2)}) collective-permute-start(bf16[1024,128]{1,0:T(8,128)(2,1)S(1)} %pad_maximum_fusion.1), channel_id=1, source_target_pairs={{0,4},{1,37},{4,32},{5,1},{32,36},{33,5},{36,0},{37,33},{2,6},{3,3... | collective-permute-start | bytes 786440 | tf_op jit(solution)/shard_map/ppermute | solution.py:301
  41.3 1.4 %collective-permute-start.3 = (bf16[512,128]{1,0:T(8,128)(2,1)S(1)}, bf16[512,128]{1,0:T(8,128)(2,1)S(1)}, u32[]{:S(2)}, u32[]{:S(2)}) collective-permute-start(bf16[512,128]{1,0:T(8,128)(2,1)S(1)} %get-tuple-element.43), channel_id=1, source_target_pairs={{0,1},{1,0},{2,3},{3,2},{4,5},{5,4},{6,7},{7,6},{8,9},{9,8},{10,11... | collective-permute-start | bytes 393224 | tf_op jit(solution)/shard_map/ppermute | solution.py:304
  45.8 4.6 %collective-permute-start.8 = (bf16[16,256,128]{2,1,0:T(8,128)(2,1)S(1)}, bf16[16,256,128]{2,1,0:T(8,128)(2,1)S(1)}, u32[]{:S(2)}, u32[]{:S(2)}) collective-permute-start(bf16[16,256,128]{2,1,0:T(8,128)(2,1)S(1)} %collective-permute-done.6.refs_1_.refs_2_), channel_id=1, source_target_pairs={{0,1},{1,0},{2,3},{3,2},{4,5},{5,4},{6,7},{7,6},{8,9},{9,8},{10,11... | collective-permute-start | bytes 3145736 | tf_op jit(solution)/shard_map/ppermute | solution.py:304
  45.9 10.5 %collective-permute-start.7 = (bf16[8,256,128]{2,1,0:T(8,128)(2,1)S(1)}, bf16[8,256,128]{2,1,0:T(8,128)(2,1)S(1)}, u32[]{:S(2)}, u32[]{:S(2)}) collective-permute-start(bf16[8,256,128]{2,1,0:T(8,128)(2,1)S(1)} %slice.19), channel_id=1, source_target_pairs={{0,8},{1,25},{8,16},{9,1},{16,24},{17,9},{24,0},{25,17},{2,10},{3,... | collective-permute-start | bytes 1572872 | tf_op jit(solution)/shard_map/ppermute | solution.py:301
  47.3 8.2 %collective-permute-start.4 = (bf16[512,128]{1,0:T(8,128)(2,1)S(1)}, bf16[512,128]{1,0:T(8,128)(2,1)S(1)}, u32[]{:S(2)}, u32[]{:S(2)}) collective-permute-start(bf16[512,128]{1,0:T(8,128)(2,1)S(1)} %get-tuple-element.44.refs_1_), channel_id=1, source_target_pairs={{0,4},{1,37},{4,32},{5,1},{32,36},{33,5},{36,0},{37,33},{2,6},{3,3... | collective-permute-start | bytes 393224 | tf_op jit(solution)/shard_map/ppermute | solution.py:301
  56.4 3.1 %collective-permute-start.9 = (bf16[8,256,128]{2,1,0:T(8,128)(2,1)S(1)}, bf16[8,256,128]{2,1,0:T(8,128)(2,1)S(1)}, u32[]{:S(2)}, u32[]{:S(2)}) collective-permute-start(bf16[8,256,128]{2,1,0:T(8,128)(2,1)S(1)} %collective-permute-done.7.refs_2_), channel_id=1, source_target_pairs={{0,1},{1,0},{2,3},{3,2},{4,5},{5,4},{6,7},{7,6},{8,9},{9,8},{10,11... | collective-permute-start | bytes 1572872 | tf_op jit(solution)/shard_map/ppermute | solution.py:304
